TPU v7x, 32 devices: a whole 2x2x4 slice. The times are simulated.
32 devices in a mesh: row: 4 (over y, x), col: 8 (over z, core).
Axes of the slice: x: 2, y: 2, z: 4, core: 2. Of those that a mesh axis runs over, the one named last changes fastest.
Arguments:
- panel_outer: bfloat16 [4, 512, 32], P('row', 'col'), may hold values from -6 to 6
- panel_inner: bfloat16 [4, 512, 32], P('row', 'col'), may hold values from -6 to 6
- upper_inner: bfloat16 [96, 512, 32], P('col', 'row'), may hold values from -0.046875 to 0.046875
- upper_outer: bfloat16 [96, 512, 32], P('col', 'row'), may hold values from -0.75 to 0.75
- tile_left: bfloat16 [4, 96, 512, 32], P('row', 'col'), may hold values from -6 to 6
- tile_right: bfloat16 [4, 96, 512, 32], P('row', 'col'), may hold values from -0.75 to 0.75
- dense_rows: bfloat16 [4, 96, 512, 512], P('row', 'col'), may hold values from -6 to 6
- tile_mask: int32 [4, 96], P('row', 'col'), may hold values 0 or 1
- start_block: float32 [64, 32], replicated, may hold values from -6 to 6
Outputs:
- updated: bfloat16 [4, 96, 512, 512], P('row', 'col')
Inputs may be any that keep to these rules, and one draw needn't show every extreme that they name: `tile_mask`: 1 marks a low-rank trailing tile, 0 a dense one.
All inputs are finite; a program needn't handle non-finite values. No bound on the sum of `tile_mask` on one device may be relied on, other than what follows from the above.
Results may differ from a plain program's by a relative error of at most 0.0039.
Values may be sent and summed in bfloat16 or wider, within the bound.
No kernel may reach another device: no remote copies, remote signals or barrier semaphores. Data moves between devices by JAX's collectives and lax.ppermute only.
A program may use at most 128 MiB of HBM per device.

v0:
```python
import jax
import jax.numpy as jnp
from jax import lax
from jax.sharding import PartitionSpec as P

ITERS = 3


HIGHEST_PRECISION = lax.Precision.HIGHEST


def orthonormalize(basis):
    gram_basis = jnp.einsum("ijna,ijnb->ijab", basis, basis, precision=HIGHEST_PRECISION)
    factor = jnp.linalg.cholesky(gram_basis)
    solved = jax.scipy.linalg.solve_triangular(factor, jnp.swapaxes(basis, -1, -2), lower=True)
    return jnp.swapaxes(solved, -1, -2)


def shards(
    panel_outer,
    panel_inner,
    upper_inner,
    upper_outer,
    tile_left,
    tile_right,
    dense_rows,
    tile_mask,
    start_block,
):
    gathered_outer, gathered_inner = (
        lax.all_gather(panel_outer, "col", axis=1, tiled=True),
        lax.all_gather(panel_inner, "col", axis=1, tiled=True),
    )
    column_inner, column_outer = (
        lax.all_gather(upper_inner, "row", axis=1, tiled=True),
        lax.all_gather(upper_outer, "row", axis=1, tiled=True),
    )
    identity = jnp.eye(2 * tile_left.shape[-1], dtype=jnp.float32)
    coupling = jnp.einsum(
        "ikr,jks->ijrs", gathered_inner, column_inner, preferred_element_type=jnp.float32
    )
    outer_float = gathered_outer.astype(jnp.float32)
    product_rows = jnp.einsum("inr,ijrs->ijns", outer_float, coupling, precision=HIGHEST_PRECISION)
    stack_rows = jnp.concatenate([tile_left.astype(jnp.float32), -product_rows], -1)
    own_block = jnp.einsum(
        "ijna,ijnb->ijab", tile_left, tile_left, preferred_element_type=jnp.float32
    )
    cross_block = jnp.einsum(
        "ijna,inb->ijab", tile_left, gathered_outer, preferred_element_type=jnp.float32
    )
    panel_block = jnp.einsum(
        "ina,inb->iab", gathered_outer, gathered_outer, preferred_element_type=jnp.float32
    )
    mixed_cross = -jnp.einsum("ijab,ijbc->ijac", cross_block, coupling, precision=HIGHEST_PRECISION)
    tail_block = jnp.einsum(
        "ijba,ibc,ijcd->ijad", coupling, panel_block, coupling, precision=HIGHEST_PRECISION
    )
    left_gram = (
        jnp.concatenate(
            [
                jnp.concatenate([own_block, mixed_cross], -1),
                jnp.concatenate([jnp.swapaxes(mixed_cross, -1, -2), tail_block], -1),
            ],
            -2,
        )
        + identity
    )
    own_right = jnp.einsum(
        "ijna,ijnb->ijab", tile_right, tile_right, preferred_element_type=jnp.float32
    )
    cross_right = jnp.einsum(
        "ijna,jnb->ijab", tile_right, column_outer, preferred_element_type=jnp.float32
    )
    panel_right = jnp.einsum(
        "jna,jnb->jab", column_outer, column_outer, preferred_element_type=jnp.float32
    )
    panel_spread = panel_right[None]
    right_gram = (
        jnp.concatenate(
            [
                jnp.concatenate([own_right, cross_right], -1),
                jnp.concatenate([jnp.swapaxes(cross_right, -1, -2), panel_spread], -1),
            ],
            -2,
        )
        + identity
    )
    factor = jnp.linalg.cholesky(left_gram)
    kernel = jnp.einsum(
        "ijba,ijbc,ijcd->ijad", factor, right_gram, factor, precision=HIGHEST_PRECISION
    )
    basis = jnp.broadcast_to(start_block, kernel.shape[:2] + start_block.shape)
    for iteration in range(ITERS):
        basis = orthonormalize(
            jnp.einsum("ijab,ijbc->ijac", kernel, basis, precision=HIGHEST_PRECISION)
        )
    projector = jnp.einsum("ijac,ijbc->ijab", basis, basis, precision=HIGHEST_PRECISION)
    middle = jnp.einsum("ijab,ijcb->ijac", projector, factor, precision=HIGHEST_PRECISION)
    solved = jax.scipy.linalg.solve_triangular(factor, jnp.swapaxes(stack_rows, -1, -2), lower=True)
    orthonormal = jnp.swapaxes(solved, -1, -2)
    combined = jnp.einsum(
        "ijna,ijab->ijnb", orthonormal, middle, precision=HIGHEST_PRECISION
    ).astype(jnp.bfloat16)
    width = tile_left.shape[-1]
    low_rows = jnp.einsum(
        "ijna,ijma->ijnm", combined[..., :width], tile_right, preferred_element_type=jnp.float32
    )
    low_rows = low_rows + jnp.einsum(
        "ijna,jma->ijnm", combined[..., width:], column_outer, preferred_element_type=jnp.float32
    )
    update = (-product_rows).astype(jnp.bfloat16)
    dense_new = dense_rows.astype(jnp.float32) + jnp.einsum(
        "ijna,jma->ijnm", update, column_outer, preferred_element_type=jnp.float32
    )
    return jnp.where((tile_mask == 1)[:, :, None, None], low_rows, dense_new).astype(jnp.bfloat16)


def solution(mesh):
    placed = (
        P("row", "col", None),
        P("row", "col", None),
        P("col", "row", None),
        P("col", "row", None),
        P("row", "col", None, None),
        P("row", "col", None, None),
        P("row", "col", None, None),
        P("row", "col"),
        P(),
    )
    return jax.shard_map(
        shards, mesh=mesh, in_specs=placed, out_specs=P("row", "col", None, None), check_vma=False
    )
```

profile of v0, /device:TPU:0, one launch (start us, length us, event | category | flops | bytes accessed | tf_op | source)
XLA Modules:
  0.0 422.5 jit_solution(11961869506967437379)
XLA Ops:
  0.0 0.7 compare_bitcast_fusion
  0.9 0.8 copy.46
  1.7 0.8 copy.48
  2.5 1.4 convolution_bitcast_fusion.4
  4.1 15.9 %all_gather.14 = bf16[1,512,32]{2,0,1:T(2,128)(2,1)S(1)} all-gather(bf16[1,64,32]{2,0,1:T(2,128)(2,1)S(1)} %copy.48), channel_id=1, replica_groups=mesh['row'=4,'col'=8] {'col'}, dimensions={1}, use_global_device_ids=true | all-gather | bytes 36864 | tf_op jit(solution)/shard_map/all_gather | solution.py:32
  20.1 14.2 %all_gather.12 = bf16[1,512,32]{2,0,1:T(2,128)(2,1)S(1)} all-gather(bf16[1,64,32]{2,0,1:T(2,128)(2,1)S(1)} %copy.46), channel_id=1, replica_groups=mesh['row'=4,'col'=8] {'col'}, dimensions={1}, use_global_device_ids=true | all-gather | bytes 36864 | tf_op jit(solution)/shard_map/all_gather | solution.py:31
  34.5 1.2 fusion.24
  35.7 10.3 %all_gather.15 = bf16[12,512,32]{1,2,0:T(8,128)(2,1)S(1)} all-gather(bf16[12,128,32]{1,2,0:T(8,128)(2,1)} %param.15), channel_id=1, replica_groups=mesh['row'=4,'col'=8] {'row'}, dimensions={1}, use_global_device_ids=true | all-gather | bytes 491520 | tf_op jit(solution)/shard_map/all_gather | solution.py:36
  46.8 8.9 %all_gather.13 = bf16[12,512,32]{1,2,0:T(8,128)(2,1)S(1)} all-gather(bf16[12,128,32]{1,2,0:T(8,128)(2,1)S(1)} %copy-done.2), channel_id=1, replica_groups=mesh['row'=4,'col'=8] {'row'}, dimensions={1}, use_global_device_ids=true | all-gather | bytes 491520 | tf_op jit(solution)/shard_map/all_gather | solution.py:35
  57.8 70.5 %custom-call.14 = f32[1,12,64,64]{3,2,1,0:T(8,128)S(1)} custom-call(f32[1,12,64,64]{3,2,1,0:T(8,128)S(1)} %fusion.23), custom_call_target="Cholesky" | custom-call | tf_op jit(solution)/shard_map/jit(cholesky)/cholesky | solution.py:88
  128.5 0.9 fusion.9
  129.4 0.6 fusion.15
  130.0 0.7 fusion.53
  131.3 35.2 %custom-call.20 = f32[1,12,32,32]{3,2,1,0:T(8,128)S(1)} custom-call(f32[1,12,32,32]{3,2,1,0:T(8,128)S(1)} %fusion.36), custom_call_target="Cholesky" | custom-call | tf_op jit(solution)/shard_map/jit(cholesky)/cholesky | solution.py:14
  166.8 29.6 %custom-call.21 = f32[12,1,32,32]{2,3,1,0:T(8,128)S(1)} custom-call(f32[12,1,32,32]{3,2,1,0:T(8,128)S(1)} %select_bitcast_fusion.3), custom_call_target="InvertDiagBlocksLowerTriangular" | custom-call | tf_op jit(solution)/shard_map/jit(_solve_triangular)/vmap()/triangular_solve | solution.py:15
  196.3 0.5 fusion.34
  196.8 0.7 fusion.70
  198.2 35.2 %custom-call.22 = f32[1,12,32,32]{3,2,1,0:T(8,128)S(1)} custom-call(f32[1,12,32,32]{3,2,1,0:T(8,128)S(1)} %fusion.33), custom_call_target="Cholesky" | custom-call | tf_op jit(solution)/shard_map/jit(cholesky)/cholesky | solution.py:14
  233.6 29.6 %custom-call.23 = f32[12,1,32,32]{2,3,1,0:T(8,128)S(1)} custom-call(f32[12,1,32,32]{3,2,1,0:T(8,128)S(1)} %select_bitcast_fusion.2), custom_call_target="InvertDiagBlocksLowerTriangular" | custom-call | tf_op jit(solution)/shard_map/jit(_solve_triangular)/vmap()/triangular_solve | solution.py:15
  263.1 0.5 fusion.31
  263.7 0.7 fusion.72
  265.0 35.2 %custom-call.24 = f32[1,12,32,32]{3,2,1,0:T(8,128)S(1)} custom-call(f32[1,12,32,32]{3,2,1,0:T(8,128)S(1)} %fusion.30), custom_call_target="Cholesky" | custom-call | tf_op jit(solution)/shard_map/jit(cholesky)/cholesky | solution.py:14
  300.4 29.6 %custom-call.25 = f32[12,1,32,32]{2,3,1,0:T(8,128)S(1)} custom-call(f32[12,1,32,32]{3,2,1,0:T(8,128)S(1)} %select_bitcast_fusion.1), custom_call_target="InvertDiagBlocksLowerTriangular" | custom-call | tf_op jit(solution)/shard_map/jit(_solve_triangular)/vmap()/triangular_solve | solution.py:15
  330.0 0.5 fusion.28
  330.5 0.8 fusion.74
  331.4 0.8 fusion.13
  332.3 59.2 %custom-call.15 = f32[12,1,64,64]{2,3,1,0:T(8,128)S(1)} custom-call(f32[12,1,64,64]{3,2,1,0:T(8,128)S(1)} %select_bitcast_fusion), custom_call_target="InvertDiagBlocksLowerTriangular" | custom-call | tf_op jit(solution)/shard_map/jit(_solve_triangular)/vmap()/triangular_solve | solution.py:99
  392.1 1.5 fusion.2
  393.6 1.5 fusion.5
  395.1 6.4 %fusion.7 = f32[12,512,512]{2,1,0:T(8,128)} fusion(bf16[12,512,32]{1,2,0:T(8,128)(2,1)S(1)} %all_gather.15, bf16[1,12,512,64]{2,3,1,0:T(8,128)(2,1)S(1)} %fusion.5), kind=kOutput, calls=%fused_computation.20 | convolution fusion | flops 201326592 | bytes 13369344 | tf_op jit(solution)/shard_map/ijna,jma->ijnm/dot_general | solution.py:108
  401.5 6.3 %fusion.8 = f32[12,512,512]{2,1,0:T(8,128)} fusion(bf16[1,12,512,64]{2,3,1,0:T(8,128)(2,1)S(1)} %fusion.5, bf16[1,12,512,32]{2,3,1,0:T(8,128)(2,1)S(1)} %copy-done), kind=kOutput, calls=%fused_computation.22 | convolution fusion | flops 201326592 | bytes 13369344 | tf_op jit(solution)/shard_map/ijna,ijma->ijnm/dot_general | solution.py:105
  407.8 14.6 %fusion.1 = bf16[1,12,512,512]{3,2,1,0:T(8,128)(2,1)} fusion(f32[12,512,512]{2,1,0:T(8,128)} %fusion.7, f32[12,512,512]{2,1,0:T(8,128)} %fusion.8, bf16[1,12,512,512]{3,2,1,0:T(8,128)(2,1)} %param.18, pred[12]{0:T(512)(128)(4,1)S(1)} %compare_bitcast_fusion, bf16[12,512,32]{1,2,0:T(8,128)(2,1)S(1)} %all_gather.15, f32[1,12,512,32]{2,3,1,0:T(8,128)S(1)} %fusion.6), kind=kOutput, calls=%fused_computation.2 | convolution fusion | flops 217251840 | bytes 38928396 | tf_op jit(solution)/shard_map/ijna,jma->ijnm/dot_general | solution.py:112
  (54 shorter events, 6.9 us)
Async XLA Ops:
  0.0 3.8 copy-start
  0.0 46.8 %copy-start.2 = (bf16[12,128,32]{1,2,0:T(8,128)(2,1)S(1)}, bf16[12,128,32]{1,2,0:T(8,128)(2,1)}, u32[]{:S(2)}) copy-start(bf16[12,128,32]{1,2,0:T(8,128)(2,1)} %param.14) | copy-start | bytes 294916
  46.2 83.7 %copy-start.3 = (f32[64,32]{0,1:T(8,128)S(1)}, f32[64,32]{0,1:T(8,128)}, u32[]{:S(2)}) copy-start(f32[64,32]{0,1:T(8,128)} %param.20) | copy-start | bytes 24580
  131.3 260.7 %copy-start.1 = (bf16[1,12,512,32]{2,3,1,0:T(8,128)(2,1)S(1)}, bf16[1,12,512,32]{2,3,1,0:T(8,128)(2,1)}, u32[]{:S(2)}) copy-start(bf16[1,12,512,32]{2,3,1,0:T(8,128)(2,1)} %param.16) | copy-start | bytes 1179652
where the time goes:
time: 423 us; the launch traced here: 422 us
  other arithmetic  326 us (77%)
  blocking collectives  49.2 us (12%)
  matrix products  43.8 us (10%)
    another operation x10, other arithmetic, orthonormalize(): factor = jnp.linalg.cholesky(gram_basis)  106 us
    another operation x7, other arithmetic, orthonormalize(): jax.scipy.linalg.solve_triangular(factor, jnp.swapaxes(basis, -1, -2), lo...  89 us
    another operation x4, other arithmetic, shards(): factor = jnp.linalg.cholesky(left_gram)  70.7 us
    another operation x3, other arithmetic, shards(): jax.scipy.linalg.solve_triangular(factor, jnp.swapaxes(stack_rows, -1, -2...  59.3 us
    all_gather x1, blocking collectives, shards(): lax.all_gather(panel_inner, 'col', axis=1, tiled=True)  15.9 us
    dot_general x1, matrix products, shards(): jnp.einsum('ijna,jma->ijnm', update, column_outer, preferred_element_type...  14.6 us
    all_gather x1, blocking collectives, shards(): lax.all_gather(panel_outer, 'col', axis=1, tiled=True)  14.2 us
    all_gather x1, blocking collectives, shards(): lax.all_gather(upper_outer, 'row', axis=1, tiled=True)  10.3 us

commit v1 on v0

v1 whole, which is shorter than its diff:
```python
import jax
import jax.numpy as jnp
from jax import lax
from jax.experimental import pallas as pl
from jax.experimental.pallas import tpu as pltpu
from jax.sharding import PartitionSpec as P

ITERS = 3
F32, BF16 = jnp.float32, jnp.bfloat16
HIGHEST = lax.Precision.HIGHEST
SLOTS = 16
GROUPS = 8
NN = (((1,), (0,)), ((), ()))
NT = (((1,), (1,)), ((), ()))
TN = (((0,), (0,)), ((), ()))


def exact(a, b, dims=NN):
    return lax.dot_general(a, b, dims, precision=HIGHEST, preferred_element_type=F32)


def plain(a, b, dims=NN):
    return lax.dot_general(a, b, dims, preferred_element_type=F32)


def split(a):
    high = a.astype(BF16)
    return high, (a - high.astype(F32)).astype(BF16)


def triple(a, b, dims=NN):
    (ah, al), (bh, bl) = split(a), split(b)
    return plain(ah, bh, dims) + (plain(ah, bl, dims) + plain(al, bh, dims))


def inverse_factors(rows_ref, result_ref):
    lane = lax.broadcasted_iota(jnp.int32, (8, 128), 1)
    sub = lax.broadcasted_iota(jnp.int32, (8, 128), 0)
    group, slot = lane // SLOTS, lane % SLOTS
    a = [[None] * 4 for _ in range(4)]
    e = [[None] * 4 for _ in range(4)]
    diag = (sub == group).astype(F32)
    zero = jnp.zeros((8, 128), F32)
    for c in range(4):
        turned = jnp.transpose(rows_ref[c * 128 : (c + 1) * 128, :])
        for jb in range(4):
            a[c][jb] = turned[jb * 8 : (jb + 1) * 8, :]
            e[c][jb] = diag if jb == c else zero
    spread = lambda x, p: jnp.broadcast_to(x[p : p + 1, :], (8, 128))
    for b in range(4):
        r, s = [], []
        for p in range(8):
            index = slot + p * SLOTS
            take = lambda x: jnp.take_along_axis(x, index, axis=1, mode="promise_in_bounds")
            r.append([take(a[b][jb]) if jb >= b else None for jb in range(4)])
            s.append([take(e[b][jb]) if jb < b else ((sub == p).astype(F32) if jb == b else None) for jb in range(4)])
        for p in range(8):
            pivot = spread(r[p][b], p)
            inverse = 1.0 / pivot
            for q in range(p + 1, 8):
                m = spread(r[q][b], p) * inverse
                for jb in range(4):
                    if jb >= b:
                        r[q][jb] = r[q][jb] - m * r[p][jb]
                    if jb <= b:
                        s[q][jb] = s[q][jb] - m * s[p][jb]
            for c in range(b, 4):
                m = spread(a[c][b], p) * inverse
                if c == b:
                    m = jnp.where(group > p, m, 0.0)
                for jb in range(4):
                    if jb >= b:
                        a[c][jb] = a[c][jb] - m * r[p][jb]
                    if jb <= b:
                        e[c][jb] = e[c][jb] - m * s[p][jb]
        pivots = jnp.sum(a[b][b] * diag, axis=0, keepdims=True)
        scale = jnp.broadcast_to(lax.rsqrt(pivots), (8, 128))
        full = jnp.concatenate([e[b][jb] * scale for jb in range(4)], axis=0)
        result_ref[b * 128 : (b + 1) * 128, :] = jnp.transpose(full)


def kernel(
    pos, mask, xy, w0, w1, w2, w3, z0, z1, z2, z3, left, right, start, dense_hbm, out_hbm,
    dense, left_rows, right_rows, turned, gram, right_gram, basis, imaged, coupling, mix, rows, factors, in_sem, out_sem,
):
    tiles, rank, order = left.shape
    r, c = pos[0], pos[1]

    def fetch(t):
        return pltpu.make_async_copy(dense_hbm.at[t], dense.at[t], in_sem.at[t])

    def drain(t):
        return pltpu.make_async_copy(dense.at[t], out_hbm.at[t], out_sem.at[t])

    for t in range(tiles):
        pl.when(mask[t] == 0)(lambda t=t: fetch(t).start())

    lanes = lax.broadcasted_iota(jnp.int32, (rank, 128), 1)
    outer, inner = [], []
    for q in range(4):
        even = xy[c ^ (2 * q)].astype(F32)
        odd = xy[c ^ (2 * q + 1)].astype(F32)
        outer.append(jnp.where(lanes < 64, even, pltpu.roll(odd, 64, 1)).astype(BF16))
        inner.append(jnp.where(lanes < 64, pltpu.roll(even, 64, 1), odd).astype(BF16))
    outer = jnp.concatenate(outer, axis=1)
    inner_all = jnp.concatenate(inner, axis=1)

    for q, (w, z) in enumerate(((w0, z0), (w1, z1), (w2, z2), (w3, z3))):
        at = pl.ds(pl.multiple_of((r ^ q) * 128, 128), 128)
        for t in range(tiles):
            right_rows[t, rank:, at] = z[t]
            turned[t, :rank, at] = w[t]
    identity = (
        lax.broadcasted_iota(jnp.int32, (64, 64), 0) == lax.broadcasted_iota(jnp.int32, (64, 64), 1)
    ).astype(F32)
    panel = plain(outer, outer, NT)
    for t in range(tiles):
        coupling[t] = plain(inner_all, turned[t, :rank, :], NT)
    for t in range(tiles):
        own = left[t]
        left_rows[t, :rank, :] = own
        left_rows[t, rank:, :] = outer
        right_rows[t, :rank, :] = right[t]
        cross = exact(plain(own, outer, NT), coupling[t])
        tail = exact(exact(coupling[t], panel, TN), coupling[t])
        gram[t] = jnp.concatenate(
            [
                jnp.concatenate([plain(own, own, NT), -cross], 1),
                jnp.concatenate([-jnp.transpose(cross), tail], 1),
            ],
            0,
        ) + identity
        right_gram[t] = plain(right_rows[t], right_rows[t], NT) + identity

    def load(t, source):
        return source[pl.ds(t, 32, SLOTS), :]

    def store(t, value):
        rows[pl.ds(t, 32, SLOTS), :] = value

    for t in range(tiles):
        store(t, gram[t, :rank, :rank])
    inverse_factors(rows, factors)
    for t in range(tiles):
        first = exact(load(t, factors), gram[t, :rank, :])
        basis[t] = exact(start[:, :rank], first)
        rest = gram[t, rank:, rank:] - exact(first[:, rank:], first[:, rank:], TN)
        imaged[t, :, :rank] = rest
        store(t, rest)
    inverse_factors(rows, factors)
    for t in range(tiles):
        second = exact(load(t, factors), imaged[t, :, :rank])
        more = exact(start[:, rank:], second)
        imaged[t] = basis[t] + jnp.concatenate([jnp.zeros((rank, rank), F32), more], 1)
    for step in range(ITERS):
        for t in range(tiles):
            moved = triple(imaged[t], right_gram[t])
            image = triple(moved, gram[t])
            basis[t] = moved
            imaged[t] = image
            store(t, exact(image, moved, NT))
        inverse_factors(rows, factors)
        for t in range(tiles):
            imaged[t] = triple(load(t, factors), imaged[t])
            if step == ITERS - 1:
                basis[t] = triple(load(t, factors), basis[t])

    for t in range(tiles):
        top = basis[t]
        tail = triple(top[:, rank:], coupling[t], NT)
        mixed = triple(jnp.concatenate([top[:, :rank], -tail], 1), imaged[t], TN)
        dense_mix = jnp.concatenate(
            [jnp.zeros((rank, 64), F32), jnp.concatenate([jnp.zeros((rank, rank), F32), -coupling[t]], 1)], 0
        )
        mix[t] = jnp.where(mask[t] == 1, mixed, dense_mix)
    for t in range(tiles):
        high, low = split(mix[t])
        combined = (plain(left_rows[t], high, TN) + plain(left_rows[t], low, TN)).astype(BF16)
        result = plain(combined, right_rows[t])

        @pl.when(mask[t] == 0)
        def _():
            fetch(t).wait()
            dense[t] = (result + dense[t].astype(F32)).astype(BF16)

        @pl.when(mask[t] != 0)
        def _():
            dense[t] = result.astype(BF16)

        drain(t).start()
    for t in range(tiles):
        drain(t).wait()


def local_step(pos, mask, xy, ws, zs, left, right, start, dense):
    tiles, rank, order = left.shape
    vmem = pl.BlockSpec(memory_space=pltpu.VMEM)
    smem = pl.BlockSpec(memory_space=pltpu.SMEM)
    hbm = pl.BlockSpec(memory_space=pl.ANY)
    small = pltpu.VMEM((tiles, rank, 2 * rank), F32)
    square = pltpu.VMEM((tiles, 2 * rank, 2 * rank), F32)
    return pl.pallas_call(
        kernel,
        out_shape=jax.ShapeDtypeStruct(dense.shape, BF16),
        in_specs=[smem, smem] + [vmem] * 12 + [hbm],
        out_specs=hbm,
        scratch_shapes=[
            pltpu.VMEM((tiles, order, order), BF16),
            pltpu.VMEM((tiles, 2 * rank, order), BF16),
            pltpu.VMEM((tiles, 2 * rank, order), BF16),
            pltpu.VMEM((tiles, rank, order), BF16),
            square,
            square,
            small,
            small,
            pltpu.VMEM((tiles, rank, rank), F32),
            square,
            pltpu.VMEM((32 * SLOTS, rank), F32),
            pltpu.VMEM((32 * SLOTS, rank), F32),
            pltpu.SemaphoreType.DMA((tiles,)),
            pltpu.SemaphoreType.DMA((tiles,)),
        ],
        compiler_params=pltpu.CompilerParams(vmem_limit_bytes=40 * 1024 * 1024),
    )(pos, mask, xy, *ws, *zs, left, right, start, dense)


def turn(x):
    return jnp.swapaxes(x, -1, -2)


def swap(x, axis, size, step):
    return lax.ppermute(x, axis, [(i, i ^ step) for i in range(size)])


def solution(mesh):
    nrow, ncol = mesh.shape["row"], mesh.shape["col"]

    def shards(
        panel_outer, panel_inner, upper_inner, upper_outer, tile_left, tile_right, dense_rows, tile_mask, start_block
    ):
        pair = jnp.concatenate([turn(panel_outer[0]), turn(panel_inner[0])], -1)
        w, z = turn(upper_inner), turn(upper_outer)
        if nrow == 4 and ncol == 8:
            pos = jnp.stack([lax.axis_index("row"), lax.axis_index("col")]).astype(jnp.int32)
            xy = jnp.stack([pair, swap(pair, "col", 8, 1)])
            ws = [w] + [swap(w, "row", 4, s) for s in (1, 2, 3)]
            zs = [z] + [swap(z, "row", 4, s) for s in (1, 2, 3)]
            xy = jnp.concatenate([xy, swap(xy, "col", 8, 2)])
            xy = jnp.concatenate([xy, swap(xy, "col", 8, 4)])
        else:
            pos = jnp.zeros((2,), jnp.int32)
            both = lax.all_gather(jnp.stack([turn(panel_outer[0]), turn(panel_inner[0])]), "col", axis=2, tiled=True)
            xy = jnp.concatenate([both[0].reshape(32, 8, 64), both[1].reshape(32, 8, 64)], -1).swapaxes(0, 1)
            w = lax.all_gather(w, "row", axis=2, tiled=True)
            z = lax.all_gather(z, "row", axis=2, tiled=True)
            ws = [w[:, :, 128 * q : 128 * q + 128] for q in range(4)]
            zs = [z[:, :, 128 * q : 128 * q + 128] for q in range(4)]
        updated = local_step(
            pos, tile_mask[0], xy, ws, zs, turn(tile_left[0]), turn(tile_right[0]), turn(start_block), dense_rows[0]
        )
        return updated[None]

    placed = (
        P("row", "col", None),
        P("row", "col", None),
        P("col", "row", None),
        P("col", "row", None),
        P("row", "col", None, None),
        P("row", "col", None, None),
        P("row", "col", None, None),
        P("row", "col"),
        P(),
    )
    return jax.shard_map(shards, mesh=mesh, in_specs=placed, out_specs=P("row", "col", None, None), check_vma=False)
```

time: 423 us -> 58.6 us (0.14)
  other arithmetic: 326 us -> 1.67 us
  blocking collectives: 49.2 us -> 0 us
  matrix products: 43.8 us -> 0 us
  Pallas kernels: 0 us -> 28.6 us
  starting transfers between devices: 0 us -> 12.8 us
  waiting for transfers between devices: 0 us -> 6.92 us
  local copies, waits for them, and re-layouts: 2.68 us -> 7.93 us
    another operation x24 -> x3, other arithmetic: 325 us -> 0.87 us  [the longest x2 0.79 us: shards(): xy = jnp.stack([pair, swap(pair, 'col', 8, 1)])]
    all_gather x4 -> x0, blocking collectives: 49.2 us -> none  [the longest x1 15.9 us: shards(): lax.all_gather(panel_inner, 'col', axis=1, tiled=True)]
    dot_general x25 -> x0, matrix products: 40.7 us -> none  [the longest x1 14.6 us: shards(): jnp.einsum('ijna,jma->ijnm', update, column_outer, preferred_element_type...]
    pallas_call x0 -> x1, Pallas kernels: none -> 28.6 us  [local_step(): pl.pallas_call(kernel, out_shape=jax.ShapeDtypeStruct(dense.shape, BF16),...]
    ppermute x0 -> x9, starting transfers between devices: none -> 12.8 us  [swap(): return lax.ppermute(x, axis, [(i, i ^ step) for i in range(size)])]
    ppermute x0 -> x9, waiting for transfers between devices: none -> 6.92 us  [swap(): return lax.ppermute(x, axis, [(i, i ^ step) for i in range(size)])]
    unnamed x10 -> x14, local copies, waits for them, and re-layouts: 1.61 us -> 7.93 us
  transfers between devices with their start and end apart: 0 -> 9, of which waited for: 0 -> 3; matrix products, arithmetic and copies ran while one was open for 0% -> 2% of each run, Pallas kernels for 0% -> 0%
where the time goes in v1:
time: 58.6 us; the launch traced here: 58.1 us
  Pallas kernels  28.6 us (49%)
  starting transfers between devices  12.8 us (22%)
  local copies, waits for them, and re-layouts  7.93 us (14%)
  waiting for transfers between devices  6.92 us (12%)
  other arithmetic  1.67 us (3%)
    pallas_call x1, Pallas kernels, local_step(): pl.pallas_call(kernel, out_shape=jax.ShapeDtypeStruct(dense.shape, BF16),...  28.6 us
    ppermute x9, starting transfers between devices, swap(): return lax.ppermute(x, axis, [(i, i ^ step) for i in range(size)])  12.8 us
    unnamed x14, local copies, waits for them, and re-layouts  7.93 us
    ppermute x9, waiting for transfers between devices, swap(): return lax.ppermute(x, axis, [(i, i ^ step) for i in range(size)])  6.92 us
  transfers between devices with their start and end apart: 9, of which 3 were waited for; matrix products, arithmetic and copies ran while one was open for 2% of the time, Pallas kernels for 0%

profile of v1, /device:TPU:0, one launch (start us, length us, event | category | flops | bytes accessed | tf_op | source)
XLA Modules:
  0.0 58.1 jit_solution(8838196714330598091)
XLA Ops:
  0.0 0.8 %pad_maximum_fusion.3 = bf16[32,128]{1,0:T(8,128)(2,1)S(1)} fusion(bf16[32,64]{1,0:T(8,128)(2,1)} %bitcast.39, bf16[32,64]{1,0:T(8,128)(2,1)} %bitcast.41), kind=kLoop, calls=%fused_computation.3 | loop fusion | flops 16384 | bytes 16384 | tf_op jit(solution)/shard_map/concatenate | solution.py:241
  0.8 0.5 collective-permute-start
  1.2 0.8 %fusion = bf16[1,32,128]{2,1,0:T(8,128)(2,1)S(1)} fusion(bf16[32,64]{1,0:T(8,128)(2,1)} %bitcast.40, bf16[32,64]{1,0:T(8,128)(2,1)} %bitcast.42), kind=kLoop, calls=%fused_computation.5 | loop fusion | flops 16384 | bytes 16384 | tf_op jit(solution)/shard_map/stack | solution.py:245
  2.0 0.0 collective-permute-done
  2.1 2.9 %collective-permute-start.1 = (bf16[2,32,128]{2,1,0:T(8,128)(2,1)S(1)}, bf16[2,32,128]{2,1,0:T(8,128)(2,1)S(1)}, u32[]{:S(2)}, u32[]{:S(2)}) collective-permute-start(bf16[2,32,128]{2,1,0:T(8,128)(2,1)S(1)} %pad_maximum_fusion.2), channel_id=1, source_target_pairs={{0,2},{1,3},{2,0},{3,1},{4,6},{5,7},{6,4},{7,5},{8,10},{9,11},{10,... | collective-permute-start | bytes 49160 | tf_op jit(solution)/shard_map/ppermute | solution.py:232
  5.0 2.4 %collective-permute-start.5 = (bf16[12,32,128]{2,1,0:T(8,128)(2,1)}, bf16[12,32,128]{2,1,0:T(8,128)(2,1)S(1)}, u32[]{:S(2)}, u32[]{:S(2)}) collective-permute-start(bf16[12,32,128]{2,1,0:T(8,128)(2,1)} %bitcast.26), channel_id=1, source_target_pairs={{0,24},{8,16},{16,8},{24,0},{1,25},{9,17},{17,9},{25,1},{2,26},{10... | collective-permute-start | bytes 294920 | tf_op jit(solution)/shard_map/ppermute | solution.py:232
  7.4 0.5 collective-permute-start.4
  7.9 0.5 collective-permute-start.3
  8.5 2.4 %collective-permute-start.8 = (bf16[12,32,128]{2,1,0:T(8,128)(2,1)}, bf16[12,32,128]{2,1,0:T(8,128)(2,1)S(1)}, u32[]{:S(2)}, u32[]{:S(2)}) collective-permute-start(bf16[12,32,128]{2,1,0:T(8,128)(2,1)} %bitcast.30), channel_id=1, source_target_pairs={{0,24},{8,16},{16,8},{24,0},{1,25},{9,17},{17,9},{25,1},{2,26},{10... | collective-permute-start | bytes 294920 | tf_op jit(solution)/shard_map/ppermute | solution.py:232
  10.9 0.0 collective-permute-done.1
  10.9 2.7 %collective-permute-start.2 = (bf16[4,32,128]{2,1,0:T(8,128)(2,1)S(1)}, bf16[4,32,128]{2,1,0:T(8,128)(2,1)S(1)}, u32[]{:S(2)}, u32[]{:S(2)}) collective-permute-start(bf16[4,32,128]{2,1,0:T(8,128)(2,1)S(1)} %pad_maximum_fusion.1), channel_id=1, source_target_pairs={{0,4},{1,5},{2,6},{3,7},{4,0},{5,1},{6,2},{7,3},{8,12},{9,13},{10,... | collective-permute-start | bytes 98312 | tf_op jit(solution)/shard_map/ppermute | solution.py:232
  13.6 0.1 pad_add_fusion.pos
  13.7 2.4 %collective-permute-done.2 = bf16[4,32,128]{2,1,0:T(8,128)(2,1)S(1)} collective-permute-done((bf16[4,32,128]{2,1,0:T(8,128)(2,1)S(1)}, bf16[4,32,128]{2,1,0:T(8,128)(2,1)S(1)}, u32[]{:S(2)}, u32[]{:S(2)}) %collective-permute-start.2) | collective-permute-done | bytes 32800 | tf_op jit(solution)/shard_map/ppermute | solution.py:232
  16.1 0.5 collective-permute-start.7
  16.6 0.0 collective-permute-done.5.w3
  16.6 0.3 collective-permute-start.6
  16.9 0.0 collective-permute-done.4.w2
  16.9 0.0 collective-permute-done.3.w1
  16.9 0.0 collective-permute-done.8.z3
  16.9 4.0 %collective-permute-done.7.z2 = bf16[12,32,128]{2,1,0:T(8,128)(2,1)S(1)} collective-permute-done((bf16[12,32,128]{2,1,0:T(8,128)(2,1)}, bf16[12,32,128]{2,1,0:T(8,128)(2,1)S(1)}, u32[]{:S(2)}, u32[]{:S(2)}) %collective-permute-start.7) | collective-permute-done | bytes 98336 | tf_op jit(solution)/shard_map/ppermute | solution.py:232
  20.9 0.5 collective-permute-done.6.z1
  21.4 0.0 copy-start
  21.4 2.8 %copy-done = bf16[1,12,512,512]{3,2,1,0:T(8,128)(2,1)S(1)} copy-done((bf16[1,12,512,512]{3,2,1,0:T(8,128)(2,1)S(1)}, bf16[1,12,512,512]{3,2,1,0:T(8,128)(2,1)}, u32[]{:S(2)}) %copy-start) | copy-done | bytes 6291480
  24.2 0.0 copy-start.1
  24.2 1.0 %copy-done.1 = bf16[1,12,512,32]{2,3,1,0:T(8,128)(2,1)S(1)} copy-done((bf16[1,12,512,32]{2,3,1,0:T(8,128)(2,1)S(1)}, bf16[1,12,512,32]{2,3,1,0:T(8,128)(2,1)}, u32[]{:S(2)}) %copy-start.1) | copy-done | bytes 393240
  25.2 0.0 copy-start.2
  25.2 1.0 %copy-done.2 = bf16[1,12,512,32]{2,3,1,0:T(8,128)(2,1)S(1)} copy-done((bf16[1,12,512,32]{2,3,1,0:T(8,128)(2,1)S(1)}, bf16[1,12,512,32]{2,3,1,0:T(8,128)(2,1)}, u32[]{:S(2)}) %copy-start.2) | copy-done | bytes 393240
  26.2 0.9 %copy-done.3 = bf16[12,128,32]{1,2,0:T(8,128)(2,1)S(1)} copy-done((bf16[12,128,32]{1,2,0:T(8,128)(2,1)S(1)}, bf16[12,128,32]{1,2,0:T(8,128)(2,1)}, u32[]{:S(2)}) %copy-start.3) | copy-done | bytes 98328
  27.1 0.9 %copy-done.4 = bf16[12,128,32]{1,2,0:T(8,128)(2,1)S(1)} copy-done((bf16[12,128,32]{1,2,0:T(8,128)(2,1)S(1)}, bf16[12,128,32]{1,2,0:T(8,128)(2,1)}, u32[]{:S(2)}) %copy-start.4) | copy-done | bytes 98328
  28.0 0.7 %copy-done.5 = f32[64,32]{0,1:T(8,128)S(1)} copy-done((f32[64,32]{0,1:T(8,128)S(1)}, f32[64,32]{0,1:T(8,128)}, u32[]{:S(2)}) %copy-start.5) | copy-done | bytes 8216
  28.7 0.7 %copy-done.6 = s32[1,12]{1,0:T(1,128)S(1)} copy-done((s32[1,12]{1,0:T(1,128)S(1)}, s32[1,12]{1,0:T(1,128)}, u32[]{:S(2)}) %copy-start.6) | copy-done | bytes 72
  29.3 28.6 %shard_map.91 = bf16[12,512,512]{2,1,0:T(8,128)(2,1)} custom-call(s32[2]{0:T(128)S(1)} %pad_add_fusion.pos, s32[12]{0:T(128)S(1)} %bitcast.35, bf16[8,32,128]{2,1,0:T(8,128)(2,1)S(1)} %pad_maximum_fusion.xy, bf16[12,32,128]{2,1,0:T(8,128)(2,1)S(1)} %bitcast.29, bf16[12,32,128]{2,1,0:T(8,128)(2,1)S(1)} %collective-permute-done.3.w1, ...), custom_call_target="tpu_custom_call" | custom-call | tf_op jit(solution)/shard_map/pallas_call | solution.py:202
  (7 shorter events, 0.0 us)
Async XLA Ops:
  0.8 1.3 %collective-permute-start = (bf16[32,128]{1,0:T(8,128)(2,1)S(1)}, bf16[32,128]{1,0:T(8,128)(2,1)S(1)}, u32[]{:S(2)}, u32[]{:S(2)}) collective-permute-start(bf16[32,128]{1,0:T(8,128)(2,1)S(1)} %pad_maximum_fusion.3), channel_id=1, source_target_pairs={{0,1},{1,0},{2,3},{3,2},{4,5},{5,4},{6,7},{7,6},{8,9},{9,8},{10,11... | collective-permute-start | bytes 24584 | tf_op jit(solution)/shard_map/ppermute | solution.py:232
  2.1 8.9 %collective-permute-start.1 = (bf16[2,32,128]{2,1,0:T(8,128)(2,1)S(1)}, bf16[2,32,128]{2,1,0:T(8,128)(2,1)S(1)}, u32[]{:S(2)}, u32[]{:S(2)}) collective-permute-start(bf16[2,32,128]{2,1,0:T(8,128)(2,1)S(1)} %pad_maximum_fusion.2), channel_id=1, source_target_pairs={{0,2},{1,3},{2,0},{3,1},{4,6},{5,7},{6,4},{7,5},{8,10},{9,11},{10,... | collective-permute-start | bytes 49160 | tf_op jit(solution)/shard_map/ppermute | solution.py:232
  5.0 11.6 %collective-permute-start.5 = (bf16[12,32,128]{2,1,0:T(8,128)(2,1)}, bf16[12,32,128]{2,1,0:T(8,128)(2,1)S(1)}, u32[]{:S(2)}, u32[]{:S(2)}) collective-permute-start(bf16[12,32,128]{2,1,0:T(8,128)(2,1)} %bitcast.26), channel_id=1, source_target_pairs={{0,24},{8,16},{16,8},{24,0},{1,25},{9,17},{17,9},{25,1},{2,26},{10... | collective-permute-start | bytes 294920 | tf_op jit(solution)/shard_map/ppermute | solution.py:232
  7.4 9.4 %collective-permute-start.4 = (bf16[12,32,128]{2,1,0:T(8,128)(2,1)}, bf16[12,32,128]{2,1,0:T(8,128)(2,1)S(1)}, u32[]{:S(2)}, u32[]{:S(2)}) collective-permute-start(bf16[12,32,128]{2,1,0:T(8,128)(2,1)} %bitcast.27), channel_id=1, source_target_pairs={{0,16},{8,24},{16,0},{24,8},{1,17},{9,25},{17,1},{25,9},{2,18},{10... | collective-permute-start | bytes 294920 | tf_op jit(solution)/shard_map/ppermute | solution.py:232
  7.9 8.9 %collective-permute-start.3 = (bf16[12,32,128]{2,1,0:T(8,128)(2,1)}, bf16[12,32,128]{2,1,0:T(8,128)(2,1)S(1)}, u32[]{:S(2)}, u32[]{:S(2)}) collective-permute-start(bf16[12,32,128]{2,1,0:T(8,128)(2,1)} %bitcast.28), channel_id=1, source_target_pairs={{0,8},{8,0},{16,24},{24,16},{1,9},{9,1},{17,25},{25,17},{2,10},{10... | collective-permute-start | bytes 294920 | tf_op jit(solution)/shard_map/ppermute | solution.py:232
  8.5 8.4 %collective-permute-start.8 = (bf16[12,32,128]{2,1,0:T(8,128)(2,1)}, bf16[12,32,128]{2,1,0:T(8,128)(2,1)S(1)}, u32[]{:S(2)}, u32[]{:S(2)}) collective-permute-start(bf16[12,32,128]{2,1,0:T(8,128)(2,1)} %bitcast.30), channel_id=1, source_target_pairs={{0,24},{8,16},{16,8},{24,0},{1,25},{9,17},{17,9},{25,1},{2,26},{10... | collective-permute-start | bytes 294920 | tf_op jit(solution)/shard_map/ppermute | solution.py:232
  10.9 5.1 %collective-permute-start.2 = (bf16[4,32,128]{2,1,0:T(8,128)(2,1)S(1)}, bf16[4,32,128]{2,1,0:T(8,128)(2,1)S(1)}, u32[]{:S(2)}, u32[]{:S(2)}) collective-permute-start(bf16[4,32,128]{2,1,0:T(8,128)(2,1)S(1)} %pad_maximum_fusion.1), channel_id=1, source_target_pairs={{0,4},{1,5},{2,6},{3,7},{4,0},{5,1},{6,2},{7,3},{8,12},{9,13},{10,... | collective-permute-start | bytes 98312 | tf_op jit(solution)/shard_map/ppermute | solution.py:232
  16.1 4.8 %collective-permute-start.7 = (bf16[12,32,128]{2,1,0:T(8,128)(2,1)}, bf16[12,32,128]{2,1,0:T(8,128)(2,1)S(1)}, u32[]{:S(2)}, u32[]{:S(2)}) collective-permute-start(bf16[12,32,128]{2,1,0:T(8,128)(2,1)} %bitcast.31), channel_id=1, source_target_pairs={{0,16},{8,24},{16,0},{24,8},{1,17},{9,25},{17,1},{25,9},{2,18},{10... | collective-permute-start | bytes 294920 | tf_op jit(solution)/shard_map/ppermute | solution.py:232
  16.6 4.8 %collective-permute-start.6 = (bf16[12,32,128]{2,1,0:T(8,128)(2,1)}, bf16[12,32,128]{2,1,0:T(8,128)(2,1)S(1)}, u32[]{:S(2)}, u32[]{:S(2)}) collective-permute-start(bf16[12,32,128]{2,1,0:T(8,128)(2,1)} %bitcast.32), channel_id=1, source_target_pairs={{0,8},{8,0},{16,24},{24,16},{1,9},{9,1},{17,25},{25,17},{2,10},{10... | collective-permute-start | bytes 294920 | tf_op jit(solution)/shard_map/ppermute | solution.py:232
  21.4 2.8 %copy-start = (bf16[1,12,512,512]{3,2,1,0:T(8,128)(2,1)S(1)}, bf16[1,12,512,512]{3,2,1,0:T(8,128)(2,1)}, u32[]{:S(2)}) copy-start(bf16[1,12,512,512]{3,2,1,0:T(8,128)(2,1)} %param.15) | copy-start | bytes 18874372
  24.2 1.0 %copy-start.1 = (bf16[1,12,512,32]{2,3,1,0:T(8,128)(2,1)S(1)}, bf16[1,12,512,32]{2,3,1,0:T(8,128)(2,1)}, u32[]{:S(2)}) copy-start(bf16[1,12,512,32]{2,3,1,0:T(8,128)(2,1)} %param.13) | copy-start | bytes 1179652
  25.2 1.0 %copy-start.2 = (bf16[1,12,512,32]{2,3,1,0:T(8,128)(2,1)S(1)}, bf16[1,12,512,32]{2,3,1,0:T(8,128)(2,1)}, u32[]{:S(2)}) copy-start(bf16[1,12,512,32]{2,3,1,0:T(8,128)(2,1)} %param.14) | copy-start | bytes 1179652
  26.2 0.9 %copy-start.3 = (bf16[12,128,32]{1,2,0:T(8,128)(2,1)S(1)}, bf16[12,128,32]{1,2,0:T(8,128)(2,1)}, u32[]{:S(2)}) copy-start(bf16[12,128,32]{1,2,0:T(8,128)(2,1)} %param.11) | copy-start | bytes 294916
  27.1 0.9 %copy-start.4 = (bf16[12,128,32]{1,2,0:T(8,128)(2,1)S(1)}, bf16[12,128,32]{1,2,0:T(8,128)(2,1)}, u32[]{:S(2)}) copy-start(bf16[12,128,32]{1,2,0:T(8,128)(2,1)} %param.12) | copy-start | bytes 294916
  28.0 0.7 %copy-start.5 = (f32[64,32]{0,1:T(8,128)S(1)}, f32[64,32]{0,1:T(8,128)}, u32[]{:S(2)}) copy-start(f32[64,32]{0,1:T(8,128)} %param.17) | copy-start | bytes 24580
  28.7 0.7 %copy-start.6 = (s32[1,12]{1,0:T(1,128)S(1)}, s32[1,12]{1,0:T(1,128)}, u32[]{:S(2)}) copy-start(s32[1,12]{1,0:T(1,128)} %param.16) | copy-start | bytes 148

commit v2 on v1

v2 whole, which is shorter than its diff:
```python
import jax
import jax.numpy as jnp
from jax import lax
from jax.experimental import pallas as pl
from jax.experimental.pallas import tpu as pltpu
from jax.sharding import PartitionSpec as P

ITERS = 3
F32, BF16 = jnp.float32, jnp.bfloat16
SLOTS = 16
GROUPS = 8
NN = (((1,), (0,)), ((), ()))
NT = (((1,), (1,)), ((), ()))
TN = (((0,), (0,)), ((), ()))


def dot(a, b, dims=NN):
    return lax.dot_general(a, b, dims, preferred_element_type=F32)


def beside(*parts):
    return jnp.concatenate(parts, axis=1)


def below(*parts):
    return jnp.concatenate(parts, axis=0)


def parts2(x):
    high = x.astype(BF16)
    return high, (x - high.astype(F32)).astype(BF16)


def parts3(x):
    high = x.astype(BF16)
    rest = x - high.astype(F32)
    middle = rest.astype(BF16)
    return high, middle, (rest - middle.astype(F32)).astype(BF16)


def pick(lanes_before, x, y):
    lane = lax.broadcasted_iota(jnp.int32, x.shape, 1)
    return jnp.where(lane < lanes_before, x.astype(F32), y.astype(F32)).astype(BF16)


def left_64(x):
    high, low = parts2(x)
    return beside(high, low[:, :64])


def right_64(x):
    high, low = parts2(x)
    return below(high, low, high)


def left_32(x):
    high, middle, low = parts3(x)
    return beside(pick(64, high, middle), pick(32, high, low)[:, :64])


def right_32(x):
    high, middle, low = parts3(x)
    return below(high, middle, high, middle, low, high)


def wide_left(x):
    high, middle, low = parts3(x)
    return beside(high, middle, pick(64, high, low))


def wide_right(x):
    high, middle, low = parts3(x)
    first = pick(64, high, middle)
    return beside(first, first, pick(64, low, high))


def inverse_factors(rows_ref, result_ref, at=0):
    lane = lax.broadcasted_iota(jnp.int32, (8, 128), 1)
    sub = lax.broadcasted_iota(jnp.int32, (8, 128), 0)
    group, slot = lane // SLOTS, lane % SLOTS
    a = [[None] * 4 for _ in range(4)]
    e = [[None] * 4 for _ in range(4)]
    diag = (sub == group).astype(F32)
    zero = jnp.zeros((8, 128), F32)
    for c in range(4):
        turned = jnp.transpose(rows_ref[c * 128 : (c + 1) * 128, :])
        for jb in range(4):
            a[c][jb] = turned[at + jb * 8 : at + (jb + 1) * 8, :]
            e[c][jb] = diag if jb == c else zero
    spread = lambda x, p: jnp.broadcast_to(x[p : p + 1, :], (8, 128))
    for b in range(4):
        r, s = [], []
        for p in range(8):
            index = slot + p * SLOTS
            take = lambda x: jnp.take_along_axis(x, index, axis=1, mode="promise_in_bounds")
            r.append([take(a[b][jb]) if jb >= b else None for jb in range(4)])
            s.append([take(e[b][jb]) if jb < b else ((sub == p).astype(F32) if jb == b else None) for jb in range(4)])
        for p in range(8):
            pivot = spread(r[p][b], p)
            inverse = 1.0 / pivot
            for q in range(p + 1, 8):
                m = spread(r[q][b], p) * inverse
                for jb in range(4):
                    if jb >= b:
                        r[q][jb] = r[q][jb] - m * r[p][jb]
                    if jb <= b:
                        s[q][jb] = s[q][jb] - m * s[p][jb]
            for c in range(b, 4):
                m = spread(a[c][b], p) * inverse
                if c == b:
                    m = jnp.where(group > p, m, 0.0)
                for jb in range(4):
                    if jb >= b:
                        a[c][jb] = a[c][jb] - m * r[p][jb]
                    if jb <= b:
                        e[c][jb] = e[c][jb] - m * s[p][jb]
        pivots = jnp.sum(a[b][b] * diag, axis=0, keepdims=True)
        scale = jnp.broadcast_to(lax.rsqrt(pivots), (8, 128))
        full = below(*[e[b][jb] * scale for jb in range(4)] * 4)
        result_ref[b * 128 : (b + 1) * 128, :] = jnp.transpose(full)


def kernel(
    pos, xy, mask_hbm, start_hbm, wz0, wz1, wz2, wz3, left, right, dense_hbm, out_hbm,
    dense, updated, left_rows, left_columns, right_rows, inner_rows, gram, gram_parts, right_parts, mixer, mixer_parts,
    raw, square, mix_parts, start, basis, imaged, image_parts, wide_rows, rows, factors, mask, load_sem, out_sem,
):
    tiles, rank, order = left.shape
    r, c = pos[0], pos[1]
    every = range(tiles)

    def drain(t):
        return pltpu.make_async_copy(updated.at[t], out_hbm.at[t], out_sem.at[t])

    loads = []
    for q, wz in enumerate((wz0, wz1, wz2, wz3)):
        at = pl.ds(pl.multiple_of((r ^ q) * 128, 128), 128)
        loads.append((wz.at[:, :rank, :], inner_rows.at[:, :, at]))
        loads.append((wz.at[:, rank:, :], right_rows.at[:, rank:, at]))
    loads.append((left, left_rows.at[:, :rank, :]))
    loads.append((right, right_rows.at[:, :rank, :]))
    loads.append((start_hbm, start))
    loads.append((mask_hbm, mask))
    loads.append((dense_hbm, dense))
    loads = [pltpu.make_async_copy(x, y, load_sem.at[i]) for i, (x, y) in enumerate(loads)]
    for copy in loads:
        copy.start()

    lanes = lax.broadcasted_iota(jnp.int32, (rank, 128), 1)
    outer, inner = [], []
    for q in range(4):
        even = xy[c ^ (2 * q)].astype(F32)
        odd = xy[c ^ (2 * q + 1)].astype(F32)
        outer.append(jnp.where(lanes < 64, even, pltpu.roll(odd, 64, 1)).astype(BF16))
        inner.append(jnp.where(lanes < 64, pltpu.roll(even, 64, 1), odd).astype(BF16))
    outer = beside(*outer)
    inner = beside(*inner)
    for t in every:
        left_rows[t, rank:, :] = outer
    for copy in loads[:-1]:
        copy.wait()

    row = lax.broadcasted_iota(jnp.int32, (64, 128), 0)
    lane = lax.broadcasted_iota(jnp.int32, (64, 128), 1)
    identity = (lane % 64 == row).astype(F32)
    tail = lane[:rank] % 64 >= rank

    coupling = dot(inner_rows[...].reshape(tiles * rank, order), below(inner, inner, inner, inner), NT)
    for t in every:
        raw[t] = dot(left_rows[t], below(left_rows[t], left_rows[t]), NT)
    for t in every:
        square[t] = dot(right_rows[t], below(right_rows[t], right_rows[t]), NT) + identity
    for t in every:
        own = -coupling[t * rank : (t + 1) * rank, :]
        mixer[t] = below(identity[:rank], jnp.where(tail, own, 0.0))
        basis[t] = dot(left_32(own), right_32(raw[t, rank:, :]))
    for t in every:
        mixer_parts[t] = right_64(mixer[t])
        right_parts[t] = right_64(square[t])
    for t in every:
        scale = wide_right(mixer[t])
        gram[t] = dot(wide_left(below(raw[t, :rank, :], basis[t])), below(scale, scale), NT) + identity
    for t in every:
        gram_parts[t] = right_64(gram[t])
        wide_rows[pl.ds(t, rank, SLOTS), :] = gram[t, :rank, :]
        left_columns[t] = jnp.transpose(below(left_rows[t], left_rows[t]))

    def inverse(t):
        return factors[pl.ds(t, rank, SLOTS), :]

    head = start[:, :rank]
    head = left_32(beside(head, head, head, head))
    foot = start[:, rank:]
    foot = left_32(beside(foot, foot, foot, foot))
    inverse_factors(wide_rows, factors)
    for t in every:
        basis[t] = dot(left_32(inverse(t)), right_32(gram[t, :rank, :]))
    for t in every:
        mix_parts[t] = right_32(basis[t])
    for t in every:
        first = mix_parts[t]
        high, middle, low = first[:32], first[32:64], first[128:160]
        square[t] = dot(below(high, high, middle, middle, high, low)[:, :64], first, TN)
    for t in every:
        imaged[t] = dot(head, mix_parts[t])
    for t in every:
        basis[t] = jnp.where(tail, gram[t, rank:, :] - square[t, rank:, :], 0.0)
        wide_rows[pl.ds(t, rank, SLOTS), :] = basis[t]
    inverse_factors(wide_rows, factors, rank)
    for t in every:
        basis[t] = dot(left_32(inverse(t)), right_32(basis[t]))
    for t in every:
        imaged[t] = imaged[t] + dot(foot, right_32(basis[t]))
    for step in range(ITERS):
        for t in every:
            basis[t] = dot(left_64(imaged[t]), right_parts[t])
        for t in every:
            imaged[t] = dot(left_64(basis[t]), gram_parts[t])
        for t in every:
            image_parts[t] = below(*parts3(imaged[t]))
            rows[pl.ds(t, rank, SLOTS), :] = dot(wide_left(imaged[t]), wide_right(basis[t]), NT)
        inverse_factors(rows, factors)
        if step < ITERS - 1:
            for t in every:
                imaged[t] = dot(inverse(t).astype(BF16)[:, :96], image_parts[t])
        else:
            for t in every:
                scale = pick(64, *parts2(inverse(t)))
                high, middle = image_parts[t, :32, :], image_parts[t, 32:64, :]
                imaged[t] = dot(scale, below(high, middle, high, middle))
                high, middle = parts2(basis[t])
                basis[t] = dot(scale, below(high, middle, high, middle))

    loads[-1].wait()
    last = (lane[:rank] % 64 == row[:rank] + rank).astype(F32)
    for t in every:
        square[t, :rank, :] = dot(left_64(basis[t]), mixer_parts[t])
    for t in every:
        admissible = mask[0, t] == 1
        high, low = parts2(jnp.where(admissible, square[t, :rank, :], mixer[t, rank:, :])[:, :64])
        raw[t] = dot(below(high, high, low), paired(jnp.where(admissible, imaged[t], last)), TN)
    for t in every:
        mix_parts[t, :128, :] = below(*parts2(raw[t]))

    def combine(t):
        return dot(left_columns[t], mix_parts[t, :128, :64]).astype(BF16)

    combined = combine(0)
    for t in every:
        admissible = mask[0, t] == 1
        following = combine(t + 1) if t + 1 < tiles else None
        for m in range(0, order, 128):
            added = jnp.where(admissible, 0.0, dense[t, m : m + 128, :].astype(F32))
            updated[t, m : m + 128, :] = (dot(combined[m : m + 128, :], right_rows[t]) + added).astype(BF16)
        drain(t).start()
        combined = following
    for t in every:
        drain(t).wait()


def paired(x):
    high, low = parts2(x)
    return below(high, low, high)


def local_step(pos, xy, mask, start, wzs, left, right, dense):
    tiles, rank, order = left.shape
    vmem = pl.BlockSpec(memory_space=pltpu.VMEM)
    smem = pl.BlockSpec(memory_space=pltpu.SMEM)
    hbm = pl.BlockSpec(memory_space=pltpu.HBM)
    free = pl.BlockSpec(memory_space=pl.ANY)
    whole = pltpu.VMEM((tiles, order, order), BF16)
    rows = pltpu.VMEM((tiles, 2 * rank, order), BF16)
    parts = pltpu.VMEM((tiles, 192, 128), BF16)
    square = pltpu.VMEM((tiles, 64, 128), F32)
    small = pltpu.VMEM((tiles, 32, 128), F32)
    return pl.pallas_call(
        kernel,
        out_shape=jax.ShapeDtypeStruct(dense.shape, BF16),
        in_specs=[smem, vmem, hbm, hbm] + [free] * 4 + [hbm] * 3,
        out_specs=hbm,
        scratch_shapes=[
            whole,
            whole,
            rows,
            pltpu.VMEM((tiles, order, 128), BF16),
            rows,
            pltpu.VMEM((tiles, rank, order), BF16),
            square,
            parts,
            parts,
            square,
            parts,
            square,
            square,
            parts,
            pltpu.VMEM((32, 64), F32),
            small,
            small,
            pltpu.VMEM((tiles, 96, 128), BF16),
            pltpu.VMEM((32 * SLOTS, 128), F32),
            pltpu.VMEM((32 * SLOTS, 32), F32),
            pltpu.VMEM((32 * SLOTS, 128), F32),
            pltpu.SMEM((1, tiles), jnp.int32),
            pltpu.SemaphoreType.DMA((13,)),
            pltpu.SemaphoreType.DMA((tiles,)),
        ],
        compiler_params=pltpu.CompilerParams(vmem_limit_bytes=56 * 1024 * 1024),
    )(pos, xy, mask, start, *wzs, left, right, dense)


def turn(x):
    return jnp.swapaxes(x, -1, -2)


def swap(x, axis, size, step):
    return lax.ppermute(x, axis, [(i, i ^ step) for i in range(size)])


def solution(mesh):
    nrow, ncol = mesh.shape["row"], mesh.shape["col"]

    def shards(
        panel_outer, panel_inner, upper_inner, upper_outer, tile_left, tile_right, dense_rows, tile_mask, start_block
    ):
        pair = jnp.concatenate([turn(panel_outer[0]), turn(panel_inner[0])], -1)
        wz = jnp.concatenate([turn(upper_inner), turn(upper_outer)], 1)
        if nrow == 4 and ncol == 8:
            pos = jnp.stack([lax.axis_index("row"), lax.axis_index("col")]).astype(jnp.int32)
            xy = jnp.stack([pair, swap(pair, "col", 8, 1)])
            wzs = [wz] + [swap(wz, "row", 4, s) for s in (1, 2, 3)]
            xy = jnp.concatenate([xy, swap(xy, "col", 8, 2)])
            xy = jnp.concatenate([xy, swap(xy, "col", 8, 4)])
        else:
            pos = jnp.zeros((2,), jnp.int32)
            both = lax.all_gather(jnp.stack([turn(panel_outer[0]), turn(panel_inner[0])]), "col", axis=2, tiled=True)
            xy = jnp.concatenate([both[0].reshape(32, 8, 64), both[1].reshape(32, 8, 64)], -1).swapaxes(0, 1)
            wz = lax.all_gather(wz, "row", axis=2, tiled=True)
            wzs = [wz[:, :, 128 * q : 128 * q + 128] for q in range(4)]
        updated = local_step(
            pos, xy, tile_mask, turn(start_block), wzs, turn(tile_left[0]), turn(tile_right[0]), dense_rows[0]
        )
        return updated[None]

    placed = (
        P("row", "col", None),
        P("row", "col", None),
        P("col", "row", None),
        P("col", "row", None),
        P("row", "col", None, None),
        P("row", "col", None, None),
        P("row", "col", None, None),
        P("row", "col"),
        P(),
    )
    return jax.shard_map(shards, mesh=mesh, in_specs=placed, out_specs=P("row", "col", None, None), check_vma=False)
```

time: 58.6 us -> 35.7 us (0.61)
  Pallas kernels: 28.6 us -> 16.7 us
  local copies, waits for them, and re-layouts: 7.93 us -> 0.66 us
  starting transfers between devices: 12.8 us -> 9.58 us
  waiting for transfers between devices: 6.92 us -> 4.59 us
  other arithmetic: 1.67 us -> 3.77 us
    pallas_call x1, Pallas kernels: 28.6 us -> 16.7 us  [local_step(): pl.pallas_call(kernel, out_shape=jax.ShapeDtypeStruct(dense.shape, BF16),...]
    unnamed x14 -> x8, local copies, waits for them, and re-layouts: 7.93 us -> 0.66 us
    ppermute x9 -> x6, starting transfers between devices: 12.8 us -> 9.58 us  [swap(): return lax.ppermute(x, axis, [(i, i ^ step) for i in range(size)])]
    ppermute x9 -> x6, waiting for transfers between devices: 6.92 us -> 4.59 us  [swap(): return lax.ppermute(x, axis, [(i, i ^ step) for i in range(size)])]
    concatenate x0 -> x1, other arithmetic: none -> 0.95 us  [shards(): wz = jnp.concatenate([turn(upper_inner), turn(upper_outer)], 1)]
    concatenate x1, other arithmetic: 0.01 us -> 0.64 us  [shards(): xy = jnp.concatenate([xy, swap(xy, 'col', 8, 4)])]
  transfers between devices with their start and end apart: 9 -> 6, of which waited for: 3 -> 3; matrix products, arithmetic and copies ran while one was open for 2% -> 8% of each run, Pallas kernels for 0% -> 0%
where the time goes in v2:
time: 35.7 us; the launch traced here: 35.3 us
  Pallas kernels  16.7 us (47%)
  starting transfers between devices  9.58 us (27%)
  waiting for transfers between devices  4.59 us (13%)
  other arithmetic  3.77 us (11%)
  local copies, waits for them, and re-layouts  0.66 us (2%)
    pallas_call x1, Pallas kernels, local_step(): pl.pallas_call(kernel, out_shape=jax.ShapeDtypeStruct(dense.shape, BF16),...  16.7 us
    ppermute x6, starting transfers between devices, swap(): return lax.ppermute(x, axis, [(i, i ^ step) for i in range(size)])  9.58 us
    ppermute x6, waiting for transfers between devices, swap(): return lax.ppermute(x, axis, [(i, i ^ step) for i in range(size)])  4.59 us
    concatenate x1, other arithmetic, shards(): wz = jnp.concatenate([turn(upper_inner), turn(upper_outer)], 1)  0.95 us
    another operation x2, other arithmetic, shards(): xy = jnp.stack([pair, swap(pair, 'col', 8, 1)])  0.79 us
    concatenate x1, other arithmetic, shards(): pair = jnp.concatenate([turn(panel_outer[0]), turn(panel_inner[0])], -1)  0.79 us
  transfers between devices with their start and end apart: 6, of which 3 were waited for; matrix products, arithmetic and copies ran while one was open for 8% of the time, Pallas kernels for 0%

profile of v2, /device:TPU:0, one launch (start us, length us, event | category | flops | bytes accessed | tf_op | source)
XLA Modules:
  0.0 35.3 jit_solution(674487654855080863)
XLA Ops:
  0.0 0.8 %pad_maximum_fusion.4 = bf16[32,128]{1,0:T(8,128)(2,1)S(1)} fusion(bf16[32,64]{1,0:T(8,128)(2,1)} %bitcast.30, bf16[32,64]{1,0:T(8,128)(2,1)} %bitcast.32), kind=kLoop, calls=%fused_computation.4 | loop fusion | flops 16384 | bytes 16384 | tf_op jit(solution)/shard_map/concatenate | solution.py:326
  0.8 0.5 %collective-permute-start = (bf16[32,128]{1,0:T(8,128)(2,1)S(1)}, bf16[32,128]{1,0:T(8,128)(2,1)S(1)}, u32[]{:S(2)}, u32[]{:S(2)}) collective-permute-start(bf16[32,128]{1,0:T(8,128)(2,1)S(1)} %pad_maximum_fusion.4), channel_id=1, source_target_pairs={{0,1},{1,0},{2,3},{3,2},{4,5},{5,4},{6,7},{7,6},{8,9},{9,8},{10,11... | collective-permute-start | bytes 24584 | tf_op jit(solution)/shard_map/ppermute | solution.py:317
  1.2 0.8 %fusion = bf16[1,32,128]{2,1,0:T(8,128)(2,1)S(1)} fusion(bf16[32,64]{1,0:T(8,128)(2,1)} %bitcast.31, bf16[32,64]{1,0:T(8,128)(2,1)} %bitcast.33), kind=kLoop, calls=%fused_computation.6 | loop fusion | flops 16384 | bytes 16384 | tf_op jit(solution)/shard_map/stack | solution.py:330
  2.0 0.0 collective-permute-done
  2.1 2.9 %collective-permute-start.1 = (bf16[2,32,128]{2,1,0:T(8,128)(2,1)S(1)}, bf16[2,32,128]{2,1,0:T(8,128)(2,1)S(1)}, u32[]{:S(2)}, u32[]{:S(2)}) collective-permute-start(bf16[2,32,128]{2,1,0:T(8,128)(2,1)S(1)} %pad_maximum_fusion.3), channel_id=1, source_target_pairs={{0,2},{1,3},{2,0},{3,1},{4,6},{5,7},{6,4},{7,5},{8,10},{9,11},{10,... | collective-permute-start | bytes 49160 | tf_op jit(solution)/shard_map/ppermute | solution.py:317
  5.0 1.0 %pad_maximum_fusion.wz0 = bf16[12,64,128]{2,1,0:T(8,128)(2,1)S(1)} fusion(bf16[12,32,128]{2,1,0:T(8,128)(2,1)} %bitcast.25, bf16[12,32,128]{2,1,0:T(8,128)(2,1)} %bitcast.26), kind=kLoop, calls=%fused_computation | loop fusion | flops 393216 | bytes 393216 | tf_op jit(solution)/shard_map/concatenate | solution.py:327
  6.0 0.0 copy-start
  6.0 2.5 %collective-permute-start.5 = (bf16[12,64,128]{2,1,0:T(8,128)(2,1)S(1)}, bf16[12,64,128]{2,1,0:T(8,128)(2,1)S(1)}, u32[]{:S(2)}, u32[]{:S(2)}) collective-permute-start(bf16[12,64,128]{2,1,0:T(8,128)(2,1)S(1)} %pad_maximum_fusion.wz0), channel_id=1, source_target_pairs={{0,24},{8,16},{16,8},{24,0},{1,25},{9,17},{17,9},{25,1},{2,26},{10... | collective-permute-start | bytes 589832 | tf_op jit(solution)/shard_map/ppermute | solution.py:317
  8.5 0.5 %collective-permute-start.4 = (bf16[12,64,128]{2,1,0:T(8,128)(2,1)S(1)}, bf16[12,64,128]{2,1,0:T(8,128)(2,1)S(1)}, u32[]{:S(2)}, u32[]{:S(2)}) collective-permute-start(bf16[12,64,128]{2,1,0:T(8,128)(2,1)S(1)} %pad_maximum_fusion.wz0), channel_id=1, source_target_pairs={{0,16},{8,24},{16,0},{24,8},{1,17},{9,25},{17,1},{25,9},{2,18},{10... | collective-permute-start | bytes 589832 | tf_op jit(solution)/shard_map/ppermute | solution.py:317
  9.0 0.5 %collective-permute-start.3 = (bf16[12,64,128]{2,1,0:T(8,128)(2,1)S(1)}, bf16[12,64,128]{2,1,0:T(8,128)(2,1)S(1)}, u32[]{:S(2)}, u32[]{:S(2)}) collective-permute-start(bf16[12,64,128]{2,1,0:T(8,128)(2,1)S(1)} %pad_maximum_fusion.wz0), channel_id=1, source_target_pairs={{0,8},{8,0},{16,24},{24,16},{1,9},{9,1},{17,25},{25,17},{2,10},{10... | collective-permute-start | bytes 589832 | tf_op jit(solution)/shard_map/ppermute | solution.py:317
  9.5 0.0 collective-permute-done.1
  9.5 2.7 %collective-permute-start.2 = (bf16[4,32,128]{2,1,0:T(8,128)(2,1)S(1)}, bf16[4,32,128]{2,1,0:T(8,128)(2,1)S(1)}, u32[]{:S(2)}, u32[]{:S(2)}) collective-permute-start(bf16[4,32,128]{2,1,0:T(8,128)(2,1)S(1)} %pad_maximum_fusion.2), channel_id=1, source_target_pairs={{0,4},{1,5},{2,6},{3,7},{4,0},{5,1},{6,2},{7,3},{8,12},{9,13},{10,... | collective-permute-start | bytes 98312 | tf_op jit(solution)/shard_map/ppermute | solution.py:317
  12.2 0.6 %pad_add_fusion.pos = s32[2]{0:T(128)} fusion(s32[1]{0:T(128)} %bitcast.1, s32[1]{0:T(128)} %bitcast), kind=kLoop, calls=%fused_computation.5 | loop fusion | flops 2 | bytes 16 | tf_op jit(solution)/shard_map/stack | solution.py:329
  12.8 1.6 %collective-permute-done.2 = bf16[4,32,128]{2,1,0:T(8,128)(2,1)S(1)} collective-permute-done((bf16[4,32,128]{2,1,0:T(8,128)(2,1)S(1)}, bf16[4,32,128]{2,1,0:T(8,128)(2,1)S(1)}, u32[]{:S(2)}, u32[]{:S(2)}) %collective-permute-start.2) | collective-permute-done | bytes 32800 | tf_op jit(solution)/shard_map/ppermute | solution.py:317
  14.4 0.6 %pad_maximum_fusion.1.xy = bf16[8,32,128]{2,1,0:T(8,128)(2,1)} fusion(bf16[4,32,128]{2,1,0:T(8,128)(2,1)S(1)} %collective-permute-done.2, bf16[2,32,128]{2,1,0:T(8,128)(2,1)S(1)} %collective-permute-done.1, bf16[1,32,128]{2,1,0:T(8,128)(2,1)S(1)} %bitcast.29, bf16[1,32,128]{2,1,0:T(8,128)(2,1)S(1)} %fusion), kind=kLoop, calls=%fused_computation.1 | loop fusion | flops 98304 | bytes 131072 | tf_op jit(solution)/shard_map/concatenate | solution.py:333
  15.1 0.0 collective-permute-done.5.wz3
  15.1 0.0 copy-start.1
  15.1 2.8 %collective-permute-done.4.wz2 = bf16[12,64,128]{2,1,0:T(8,128)(2,1)S(1)} collective-permute-done((bf16[12,64,128]{2,1,0:T(8,128)(2,1)S(1)}, bf16[12,64,128]{2,1,0:T(8,128)(2,1)S(1)}, u32[]{:S(2)}, u32[]{:S(2)}) %collective-permute-start.4) | collective-permute-done | bytes 196640 | tf_op jit(solution)/shard_map/ppermute | solution.py:317
  17.9 0.0 copy-start.2
  17.9 0.1 collective-permute-done.3.wz1
  18.0 0.0 copy-start.3
  18.0 0.0 copy-done
  18.0 0.0 copy-done.1
  18.0 0.6 %copy-done.2 = bf16[12,64,128]{2,1,0:T(8,128)(2,1)} copy-done((bf16[12,64,128]{2,1,0:T(8,128)(2,1)}, bf16[12,64,128]{2,1,0:T(8,128)(2,1)S(1)}, u32[]{:S(2)}) %copy-start.2) | copy-done | bytes 196632
  18.5 0.1 copy-done.3
  18.6 16.7 %shard_map.91 = bf16[12,512,512]{2,1,0:T(8,128)(2,1)} custom-call(s32[2]{0:T(128)} %pad_add_fusion.pos, bf16[8,32,128]{2,1,0:T(8,128)(2,1)} %pad_maximum_fusion.1.xy, s32[1,12]{1,0:T(1,128)} %mask_hbm.1, f32[32,64]{1,0:T(8,128)} %bitcast.34, bf16[12,64,128]{2,1,0:T(8,128)(2,1)} %copy-done, bf16[12,64,128]{2,1,0:T(8,128)(2,1)} %copy-done.3, ...), custom_call_target="tpu_custom_call" | custom-call | tf_op jit(solution)/shard_map/pallas_call | solution.py:277
  (2 shorter events, 0.0 us)
Async XLA Ops:
  0.8 1.3 %collective-permute-start = (bf16[32,128]{1,0:T(8,128)(2,1)S(1)}, bf16[32,128]{1,0:T(8,128)(2,1)S(1)}, u32[]{:S(2)}, u32[]{:S(2)}) collective-permute-start(bf16[32,128]{1,0:T(8,128)(2,1)S(1)} %pad_maximum_fusion.4), channel_id=1, source_target_pairs={{0,1},{1,0},{2,3},{3,2},{4,5},{5,4},{6,7},{7,6},{8,9},{9,8},{10,11... | collective-permute-start | bytes 24584 | tf_op jit(solution)/shard_map/ppermute | solution.py:317
  2.1 7.4 %collective-permute-start.1 = (bf16[2,32,128]{2,1,0:T(8,128)(2,1)S(1)}, bf16[2,32,128]{2,1,0:T(8,128)(2,1)S(1)}, u32[]{:S(2)}, u32[]{:S(2)}) collective-permute-start(bf16[2,32,128]{2,1,0:T(8,128)(2,1)S(1)} %pad_maximum_fusion.3), channel_id=1, source_target_pairs={{0,2},{1,3},{2,0},{3,1},{4,6},{5,7},{6,4},{7,5},{8,10},{9,11},{10,... | collective-permute-start | bytes 49160 | tf_op jit(solution)/shard_map/ppermute | solution.py:317
  6.0 12.0 %copy-start = (bf16[12,64,128]{2,1,0:T(8,128)(2,1)}, bf16[12,64,128]{2,1,0:T(8,128)(2,1)S(1)}, u32[]{:S(2)}) copy-start(bf16[12,64,128]{2,1,0:T(8,128)(2,1)S(1)} %pad_maximum_fusion.wz0) | copy-start | bytes 589828
  6.0 9.1 %collective-permute-start.5 = (bf16[12,64,128]{2,1,0:T(8,128)(2,1)S(1)}, bf16[12,64,128]{2,1,0:T(8,128)(2,1)S(1)}, u32[]{:S(2)}, u32[]{:S(2)}) collective-permute-start(bf16[12,64,128]{2,1,0:T(8,128)(2,1)S(1)} %pad_maximum_fusion.wz0), channel_id=1, source_target_pairs={{0,24},{8,16},{16,8},{24,0},{1,25},{9,17},{17,9},{25,1},{2,26},{10... | collective-permute-start | bytes 589832 | tf_op jit(solution)/shard_map/ppermute | solution.py:317
  8.5 9.4 %collective-permute-start.4 = (bf16[12,64,128]{2,1,0:T(8,128)(2,1)S(1)}, bf16[12,64,128]{2,1,0:T(8,128)(2,1)S(1)}, u32[]{:S(2)}, u32[]{:S(2)}) collective-permute-start(bf16[12,64,128]{2,1,0:T(8,128)(2,1)S(1)} %pad_maximum_fusion.wz0), channel_id=1, source_target_pairs={{0,16},{8,24},{16,0},{24,8},{1,17},{9,25},{17,1},{25,9},{2,18},{10... | collective-permute-start | bytes 589832 | tf_op jit(solution)/shard_map/ppermute | solution.py:317
  9.0 9.0 %collective-permute-start.3 = (bf16[12,64,128]{2,1,0:T(8,128)(2,1)S(1)}, bf16[12,64,128]{2,1,0:T(8,128)(2,1)S(1)}, u32[]{:S(2)}, u32[]{:S(2)}) collective-permute-start(bf16[12,64,128]{2,1,0:T(8,128)(2,1)S(1)} %pad_maximum_fusion.wz0), channel_id=1, source_target_pairs={{0,8},{8,0},{16,24},{24,16},{1,9},{9,1},{17,25},{25,17},{2,10},{10... | collective-permute-start | bytes 589832 | tf_op jit(solution)/shard_map/ppermute | solution.py:317
  9.5 4.9 %collective-permute-start.2 = (bf16[4,32,128]{2,1,0:T(8,128)(2,1)S(1)}, bf16[4,32,128]{2,1,0:T(8,128)(2,1)S(1)}, u32[]{:S(2)}, u32[]{:S(2)}) collective-permute-start(bf16[4,32,128]{2,1,0:T(8,128)(2,1)S(1)} %pad_maximum_fusion.2), channel_id=1, source_target_pairs={{0,4},{1,5},{2,6},{3,7},{4,0},{5,1},{6,2},{7,3},{8,12},{9,13},{10,... | collective-permute-start | bytes 98312 | tf_op jit(solution)/shard_map/ppermute | solution.py:317
  15.1 2.9 %copy-start.1 = (bf16[12,64,128]{2,1,0:T(8,128)(2,1)}, bf16[12,64,128]{2,1,0:T(8,128)(2,1)S(1)}, u32[]{:S(2)}) copy-start(bf16[12,64,128]{2,1,0:T(8,128)(2,1)S(1)} %collective-permute-done.5.wz3) | copy-start | bytes 589828
  17.9 0.7 %copy-start.2 = (bf16[12,64,128]{2,1,0:T(8,128)(2,1)}, bf16[12,64,128]{2,1,0:T(8,128)(2,1)S(1)}, u32[]{:S(2)}) copy-start(bf16[12,64,128]{2,1,0:T(8,128)(2,1)S(1)} %collective-permute-done.4.wz2) | copy-start | bytes 589828
  18.0 0.7 %copy-start.3 = (bf16[12,64,128]{2,1,0:T(8,128)(2,1)}, bf16[12,64,128]{2,1,0:T(8,128)(2,1)S(1)}, u32[]{:S(2)}) copy-start(bf16[12,64,128]{2,1,0:T(8,128)(2,1)S(1)} %collective-permute-done.3.wz1) | copy-start | bytes 589828

commit v3 on v2

--- a/solution.py
+++ b/solution.py
@@ -1,3 +1,5 @@
+import functools
+
 import jax
 import jax.numpy as jnp
 from jax import lax
@@ -8,7 +10,6 @@
 ITERS = 3
 F32, BF16 = jnp.float32, jnp.bfloat16
 SLOTS = 16
-GROUPS = 8
 NN = (((1,), (0,)), ((), ()))
 NT = (((1,), (1,)), ((), ()))
 TN = (((0,), (0,)), ((), ()))
@@ -75,58 +76,60 @@
 
 
 def inverse_factors(rows_ref, result_ref, at=0):
-    lane = lax.broadcasted_iota(jnp.int32, (8, 128), 1)
-    sub = lax.broadcasted_iota(jnp.int32, (8, 128), 0)
-    group, slot = lane // SLOTS, lane % SLOTS
-    a = [[None] * 4 for _ in range(4)]
-    e = [[None] * 4 for _ in range(4)]
-    diag = (sub == group).astype(F32)
-    zero = jnp.zeros((8, 128), F32)
-    for c in range(4):
-        turned = jnp.transpose(rows_ref[c * 128 : (c + 1) * 128, :])
-        for jb in range(4):
-            a[c][jb] = turned[at + jb * 8 : at + (jb + 1) * 8, :]
-            e[c][jb] = diag if jb == c else zero
-    spread = lambda x, p: jnp.broadcast_to(x[p : p + 1, :], (8, 128))
+    sub = lax.broadcasted_iota(jnp.int32, (8, SLOTS), 0)
+    one = [(sub == p).astype(F32) for p in range(8)]
+    a = []
+    for i in range(32):
+        turned = jnp.transpose(rows_ref[i * SLOTS : (i + 1) * SLOTS, :])
+        a.append({jb: turned[at + jb * 8 : at + jb * 8 + 8, :] for jb in range(i // 8, 4)})
+    e = [{i // 8: one[i % 8]} for i in range(32)]
+
+    def spread(x, p):
+        return jnp.broadcast_to(x[p : p + 1, :], (8, SLOTS))
+
+    def less(x, m, y):
+        return -(m * y) if x is None else x - m * y
+
     for b in range(4):
-        r, s = [], []
+        r, s = a[8 * b : 8 * b + 8], e[8 * b : 8 * b + 8]
+        d = [[spread(r[p][b], q) for p in range(q + 1)] for q in range(8)]
+        m = [[None] * 8 for _ in range(8)]
+        inverse = []
         for p in range(8):
-            index = slot + p * SLOTS
-            take = lambda x: jnp.take_along_axis(x, index, axis=1, mode="promise_in_bounds")
-            r.append([take(a[b][jb]) if jb >= b else None for jb in range(4)])
-            s.append([take(e[b][jb]) if jb < b else ((sub == p).astype(F32) if jb == b else None) for jb in range(4)])
+            inverse.append(1.0 / d[p][p])
+            for q in range(p + 1, 8):
+                m[q][p] = d[q][p] * inverse[p]
+                for w in range(p + 1, q + 1):
+                    d[q][w] = d[q][w] - m[q][p] * d[w][p]
         for p in range(8):
-            pivot = spread(r[p][b], p)
-            inverse = 1.0 / pivot
             for q in range(p + 1, 8):
-                m = spread(r[q][b], p) * inverse
-                for jb in range(4):
-                    if jb >= b:
-                        r[q][jb] = r[q][jb] - m * r[p][jb]
-                    if jb <= b:
-                        s[q][jb] = s[q][jb] - m * s[p][jb]
-            for c in range(b, 4):
-                m = spread(a[c][b], p) * inverse
-                if c == b:
-                    m = jnp.where(group > p, m, 0.0)
-                for jb in range(4):
-                    if jb >= b:
-                        a[c][jb] = a[c][jb] - m * r[p][jb]
-                    if jb <= b:
-                        e[c][jb] = e[c][jb] - m * s[p][jb]
-        pivots = jnp.sum(a[b][b] * diag, axis=0, keepdims=True)
-        scale = jnp.broadcast_to(lax.rsqrt(pivots), (8, 128))
-        full = below(*[e[b][jb] * scale for jb in range(4)] * 4)
-        result_ref[b * 128 : (b + 1) * 128, :] = jnp.transpose(full)
+                for jb in range(b + 1, 4):
+                    r[q][jb] = r[q][jb] - m[q][p] * r[p][jb]
+                for jb in range(b + 1):
+                    s[q][jb] = s[q][jb] - m[q][p] * s[p][jb]
+        for c in range(b + 1, 4):
+            scaled = [r[p][c] * inverse[p] for p in range(8)]
+            for i in range(8 * c, 8 * c + 8):
+                for p in range(8):
+                    k = spread(scaled[p], i % 8)
+                    for jb in range(c, 4):
+                        a[i][jb] = a[i][jb] - k * r[p][jb]
+                    for jb in range(b + 1):
+                        e[i][jb] = less(e[i].get(jb), k, s[p][jb])
+        for p in range(8):
+            scale = lax.rsqrt(d[p][p])
+            full = below(*[s[p][jb] * scale for jb in range(b + 1)], *[jnp.zeros((8, SLOTS), F32)] * (3 - b))
+            i = 8 * b + p
+            result_ref[i * SLOTS : (i + 1) * SLOTS, :] = jnp.transpose(below(full, full, full, full))
 
 
 def kernel(
-    pos, xy, mask_hbm, start_hbm, wz0, wz1, wz2, wz3, left, right, dense_hbm, out_hbm,
+    place, near, far, mask_hbm, start_hbm, wz0, wz1, wz2, wz3, left, right, dense_hbm, out_hbm,
     dense, updated, left_rows, left_columns, right_rows, inner_rows, gram, gram_parts, right_parts, mixer, mixer_parts,
     raw, square, mix_parts, start, basis, imaged, image_parts, wide_rows, rows, factors, mask, load_sem, out_sem,
 ):
     tiles, rank, order = left.shape
-    r, c = pos[0], pos[1]
+    r, c = place()
     every = range(tiles)
 
     def drain(t):
@@ -149,8 +152,9 @@
     lanes = lax.broadcasted_iota(jnp.int32, (rank, 128), 1)
     outer, inner = [], []
     for q in range(4):
-        even = xy[c ^ (2 * q)].astype(F32)
-        odd = xy[c ^ (2 * q + 1)].astype(F32)
+        even, odd = [
+            jnp.where((c ^ p) < 4, near[(c ^ p) % 4].astype(F32), far[(c ^ p) % 4].astype(F32)) for p in (2 * q, 2 * q + 1)
+        ]
         outer.append(jnp.where(lanes < 64, even, pltpu.roll(odd, 64, 1)).astype(BF16))
         inner.append(jnp.where(lanes < 64, pltpu.roll(even, 64, 1), odd).astype(BF16))
     outer = beside(*outer)
@@ -190,7 +194,7 @@
 
     head = start[:, :rank]
     head = left_32(beside(head, head, head, head))
-    foot = start[:, rank:]
+    foot = start[:, rank : 2 * rank]
     foot = left_32(beside(foot, foot, foot, foot))
     inverse_factors(wide_rows, factors)
     for t in every:
@@ -263,10 +267,9 @@
     return below(high, low, high)
 
 
-def local_step(pos, xy, mask, start, wzs, left, right, dense):
+def local_step(place, near, far, mask, start, wzs, left, right, dense):
     tiles, rank, order = left.shape
     vmem = pl.BlockSpec(memory_space=pltpu.VMEM)
-    smem = pl.BlockSpec(memory_space=pltpu.SMEM)
     hbm = pl.BlockSpec(memory_space=pltpu.HBM)
     free = pl.BlockSpec(memory_space=pl.ANY)
     whole = pltpu.VMEM((tiles, order, order), BF16)
@@ -275,9 +278,9 @@
     square = pltpu.VMEM((tiles, 64, 128), F32)
     small = pltpu.VMEM((tiles, 32, 128), F32)
     return pl.pallas_call(
-        kernel,
+        functools.partial(kernel, place),
         out_shape=jax.ShapeDtypeStruct(dense.shape, BF16),
-        in_specs=[smem, vmem, hbm, hbm] + [free] * 4 + [hbm] * 3,
+        in_specs=[vmem, vmem, free, free] + [free] * 4 + [hbm] * 3,
         out_specs=hbm,
         scratch_shapes=[
             whole,
@@ -294,7 +297,7 @@
             square,
             square,
             parts,
-            pltpu.VMEM((32, 64), F32),
+            pltpu.VMEM((32, 128), F32),
             small,
             small,
             pltpu.VMEM((tiles, 96, 128), BF16),
@@ -305,8 +308,8 @@
             pltpu.SemaphoreType.DMA((13,)),
             pltpu.SemaphoreType.DMA((tiles,)),
         ],
-        compiler_params=pltpu.CompilerParams(vmem_limit_bytes=56 * 1024 * 1024),
-    )(pos, xy, mask, start, *wzs, left, right, dense)
+        compiler_params=pltpu.CompilerParams(vmem_limit_bytes=53 * 1024 * 1024),
+    )(near, far, mask, start, *wzs, left, right, dense)
 
 
 def turn(x):
@@ -326,19 +329,23 @@
         pair = jnp.concatenate([turn(panel_outer[0]), turn(panel_inner[0])], -1)
         wz = jnp.concatenate([turn(upper_inner), turn(upper_outer)], 1)
         if nrow == 4 and ncol == 8:
-            pos = jnp.stack([lax.axis_index("row"), lax.axis_index("col")]).astype(jnp.int32)
-            xy = jnp.stack([pair, swap(pair, "col", 8, 1)])
+            place = lambda: (lax.axis_index("row"), lax.axis_index("col"))
+            pair, wz = lax.optimization_barrier((pair, wz))
+            near = jnp.stack([pair, swap(pair, "col", 8, 1)])
             wzs = [wz] + [swap(wz, "row", 4, s) for s in (1, 2, 3)]
-            xy = jnp.concatenate([xy, swap(xy, "col", 8, 2)])
-            xy = jnp.concatenate([xy, swap(xy, "col", 8, 4)])
+            near = jnp.concatenate([near, swap(near, "col", 8, 2)])
+            far = swap(near, "col", 8, 4)
         else:
-            pos = jnp.zeros((2,), jnp.int32)
+            place = lambda: (0, 0)
             both = lax.all_gather(jnp.stack([turn(panel_outer[0]), turn(panel_inner[0])]), "col", axis=2, tiled=True)
             xy = jnp.concatenate([both[0].reshape(32, 8, 64), both[1].reshape(32, 8, 64)], -1).swapaxes(0, 1)
+            near, far = xy[:4], xy[4:]
             wz = lax.all_gather(wz, "row", axis=2, tiled=True)
             wzs = [wz[:, :, 128 * q : 128 * q + 128] for q in range(4)]
+        flags = (tile_mask == 1).astype(jnp.int32)
+        start = jnp.concatenate([turn(start_block), turn(start_block)], 1)
         updated = local_step(
-            pos, xy, tile_mask, turn(start_block), wzs, turn(tile_left[0]), turn(tile_right[0]), dense_rows[0]
+            place, near, far, flags, start, wzs, turn(tile_left[0]), turn(tile_right[0]), dense_rows[0]
         )
         return updated[None]
 

time: 35.7 us -> 31.4 us (0.88)
  waiting for transfers between devices: 4.59 us -> 2.87 us
  Pallas kernels: 16.7 us -> 15.1 us
  local copies, waits for them, and re-layouts: 0.66 us -> 0 us
  other arithmetic: 3.77 us -> 3.28 us
    ppermute x6, waiting for transfers between devices: 4.59 us -> 2.87 us  [swap(): return lax.ppermute(x, axis, [(i, i ^ step) for i in range(size)])]
    pallas_call x1, Pallas kernels: 16.7 us -> 15.1 us  [local_step(): pl.pallas_call(functools.partial(kernel, place), out_shape=jax.ShapeDtype...]
    another operation x3 -> x1, other arithmetic: 1.38 us -> 0.01 us  [shards(): near = jnp.stack([pair, swap(pair, 'col', 8, 1)])]
    unnamed x8 -> x0, local copies, waits for them, and re-layouts: 0.66 us -> none
    convert_element_type x0 -> x1, other arithmetic: none -> 0.66 us  [shards(): flags = (tile_mask == 1).astype(jnp.int32)]
  transfers between devices with their start and end apart: 6 -> 6, of which waited for: 3 -> 4; matrix products, arithmetic and copies ran while one was open for 8% -> 5% of each run, Pallas kernels for 0% -> 0%
where the time goes in v3:
time: 31.4 us; the launch traced here: 30.9 us
  Pallas kernels  15.1 us (48%)
  starting transfers between devices  9.64 us (31%)
  other arithmetic  3.28 us (10%)
  waiting for transfers between devices  2.87 us (9%)
    pallas_call x1, Pallas kernels, local_step(): pl.pallas_call(functools.partial(kernel, place), out_shape=jax.ShapeDtype...  15.1 us
    ppermute x6, starting transfers between devices, swap(): return lax.ppermute(x, axis, [(i, i ^ step) for i in range(size)])  9.64 us
    ppermute x6, waiting for transfers between devices, swap(): return lax.ppermute(x, axis, [(i, i ^ step) for i in range(size)])  2.87 us
    concatenate x1, other arithmetic, shards(): wz = jnp.concatenate([turn(upper_inner), turn(upper_outer)], 1)  0.96 us
    concatenate x1, other arithmetic, shards(): start = jnp.concatenate([turn(start_block), turn(start_block)], 1)  0.87 us
    concatenate x1, other arithmetic, shards(): pair = jnp.concatenate([turn(panel_outer[0]), turn(panel_inner[0])], -1)  0.79 us
    convert_element_type x1, other arithmetic, shards(): flags = (tile_mask == 1).astype(jnp.int32)  0.66 us
  transfers between devices with their start and end apart: 6, of which 4 were waited for; matrix products, arithmetic and copies ran while one was open for 5% of the time, Pallas kernels for 0%

profile of v3, /device:TPU:0, one launch (start us, length us, event | category | flops | bytes accessed | tf_op | source)
XLA Modules:
  0.0 30.9 jit_solution(5359333956124790703)
XLA Ops:
  0.0 0.8 %pad_maximum_fusion.4 = bf16[32,128]{1,0:T(8,128)(2,1)S(1)} fusion(bf16[32,64]{1,0:T(8,128)(2,1)} %bitcast.29, bf16[32,64]{1,0:T(8,128)(2,1)} %bitcast.30), kind=kLoop, calls=%fused_computation.4 | loop fusion | flops 16384 | bytes 16384 | tf_op jit(solution)/shard_map/concatenate | solution.py:329
  0.8 1.0 %pad_maximum_fusion.wz0 = bf16[12,64,128]{2,1,0:T(8,128)(2,1)S(1)} fusion(bf16[12,32,128]{2,1,0:T(8,128)(2,1)} %bitcast.22, bf16[12,32,128]{2,1,0:T(8,128)(2,1)} %bitcast.23), kind=kLoop, calls=%fused_computation | loop fusion | flops 393216 | bytes 393216 | tf_op jit(solution)/shard_map/concatenate | solution.py:330
  1.8 0.5 %collective-permute-start = (bf16[32,128]{1,0:T(8,128)(2,1)S(1)}, bf16[32,128]{1,0:T(8,128)(2,1)S(1)}, u32[]{:S(2)}, u32[]{:S(2)}) collective-permute-start(bf16[32,128]{1,0:T(8,128)(2,1)S(1)} %pad_maximum_fusion.4), channel_id=1, source_target_pairs={{0,1},{1,0},{2,3},{3,2},{4,5},{5,4},{6,7},{7,6},{8,9},{9,8},{10,11... | collective-permute-start | bytes 24584 | tf_op jit(solution)/shard_map/ppermute | solution.py:320
  2.3 3.5 %collective-permute-start.5 = (bf16[12,64,128]{2,1,0:T(8,128)(2,1)S(1)}, bf16[12,64,128]{2,1,0:T(8,128)(2,1)S(1)}, u32[]{:S(2)}, u32[]{:S(2)}) collective-permute-start(bf16[12,64,128]{2,1,0:T(8,128)(2,1)S(1)} %pad_maximum_fusion.wz0), channel_id=1, source_target_pairs={{0,24},{8,16},{16,8},{24,0},{1,25},{9,17},{17,9},{25,1},{2,26},{10... | collective-permute-start | bytes 589832 | tf_op jit(solution)/shard_map/ppermute | solution.py:320
  5.8 0.5 %collective-permute-start.4 = (bf16[12,64,128]{2,1,0:T(8,128)(2,1)S(1)}, bf16[12,64,128]{2,1,0:T(8,128)(2,1)S(1)}, u32[]{:S(2)}, u32[]{:S(2)}) collective-permute-start(bf16[12,64,128]{2,1,0:T(8,128)(2,1)S(1)} %pad_maximum_fusion.wz0), channel_id=1, source_target_pairs={{0,16},{8,24},{16,0},{24,8},{1,17},{9,25},{17,1},{25,9},{2,18},{10... | collective-permute-start | bytes 589832 | tf_op jit(solution)/shard_map/ppermute | solution.py:320
  6.3 0.1 collective-permute-start.3
  6.4 0.0 collective-permute-done
  6.4 2.0 %collective-permute-start.1 = (bf16[2,32,128]{2,1,0:T(8,128)(2,1)S(1)}, bf16[2,32,128]{2,1,0:T(8,128)(2,1)S(1)}, u32[]{:S(2)}, u32[]{:S(2)}) collective-permute-start(bf16[2,32,128]{2,1,0:T(8,128)(2,1)S(1)} %pad_maximum_fusion.2), channel_id=1, source_target_pairs={{0,2},{1,3},{2,0},{3,1},{4,6},{5,7},{6,4},{7,5},{8,10},{9,11},{10,... | collective-permute-start | bytes 49160 | tf_op jit(solution)/shard_map/ppermute | solution.py:320
  8.4 0.7 %compare_convert_fusion.mask_hbm = s32[1,12]{1,0:T(1,128)S(1)} fusion(s32[1,12]{1,0:T(1,128)} %param.16), kind=kLoop, calls=%fused_computation.5 | loop fusion | flops 24 | bytes 96 | tf_op jit(solution)/shard_map/convert_element_type | solution.py:345
  9.1 1.1 %collective-permute-done.1 = bf16[2,32,128]{2,1,0:T(8,128)(2,1)S(1)} collective-permute-done((bf16[2,32,128]{2,1,0:T(8,128)(2,1)S(1)}, bf16[2,32,128]{2,1,0:T(8,128)(2,1)S(1)}, u32[]{:S(2)}, u32[]{:S(2)}) %collective-permute-start.1) | collective-permute-done | bytes 16416 | tf_op jit(solution)/shard_map/ppermute | solution.py:320
  10.2 3.0 %collective-permute-start.2 = (bf16[4,32,128]{2,1,0:T(8,128)(2,1)S(1)}, bf16[4,32,128]{2,1,0:T(8,128)(2,1)S(1)}, u32[]{:S(2)}, u32[]{:S(2)}) collective-permute-start(bf16[4,32,128]{2,1,0:T(8,128)(2,1)S(1)} %pad_maximum_fusion.1.near), channel_id=1, source_target_pairs={{0,4},{1,5},{2,6},{3,7},{4,0},{5,1},{6,2},{7,3},{8,12},{9,13},{10,... | collective-permute-start | bytes 98312 | tf_op jit(solution)/shard_map/ppermute | solution.py:320
  13.2 0.9 %pad_maximum_fusion.3.start_hbm = f32[32,128]{1,0:T(8,128)S(1)} fusion(f32[32,64]{1,0:T(8,128)} %bitcast.28), kind=kLoop, calls=%fused_computation.3 | loop fusion | flops 4096 | bytes 24576 | tf_op jit(solution)/shard_map/concatenate | solution.py:346
  14.0 1.0 %collective-permute-done.2.far = bf16[4,32,128]{2,1,0:T(8,128)(2,1)S(1)} collective-permute-done((bf16[4,32,128]{2,1,0:T(8,128)(2,1)S(1)}, bf16[4,32,128]{2,1,0:T(8,128)(2,1)S(1)}, u32[]{:S(2)}, u32[]{:S(2)}) %collective-permute-start.2) | collective-permute-done | bytes 32800 | tf_op jit(solution)/shard_map/ppermute | solution.py:320
  15.1 0.0 collective-permute-done.5.wz3
  15.1 0.4 %collective-permute-done.4.wz2 = bf16[12,64,128]{2,1,0:T(8,128)(2,1)S(1)} collective-permute-done((bf16[12,64,128]{2,1,0:T(8,128)(2,1)S(1)}, bf16[12,64,128]{2,1,0:T(8,128)(2,1)S(1)}, u32[]{:S(2)}, u32[]{:S(2)}) %collective-permute-start.4) | collective-permute-done | bytes 196640 | tf_op jit(solution)/shard_map/ppermute | solution.py:320
  15.5 0.3 %collective-permute-done.3.wz1 = bf16[12,64,128]{2,1,0:T(8,128)(2,1)S(1)} collective-permute-done((bf16[12,64,128]{2,1,0:T(8,128)(2,1)S(1)}, bf16[12,64,128]{2,1,0:T(8,128)(2,1)S(1)}, u32[]{:S(2)}, u32[]{:S(2)}) %collective-permute-start.3) | collective-permute-done | bytes 196640 | tf_op jit(solution)/shard_map/ppermute | solution.py:320
  15.8 15.1 %shard_map.91 = bf16[12,512,512]{2,1,0:T(8,128)(2,1)} custom-call(bf16[4,32,128]{2,1,0:T(8,128)(2,1)S(1)} %pad_maximum_fusion.1.near, bf16[4,32,128]{2,1,0:T(8,128)(2,1)S(1)} %collective-permute-done.2.far, s32[1,12]{1,0:T(1,128)S(1)} %compare_convert_fusion.mask_hbm, f32[32,128]{1,0:T(8,128)S(1)} %pad_maximum_fusion.3.start_hbm, ...), custom_call_target="tpu_custom_call" | custom-call | tf_op jit(solution)/shard_map/pallas_call | solution.py:280
  (2 shorter events, 0.0 us)
Async XLA Ops:
  1.8 4.7 %collective-permute-start = (bf16[32,128]{1,0:T(8,128)(2,1)S(1)}, bf16[32,128]{1,0:T(8,128)(2,1)S(1)}, u32[]{:S(2)}, u32[]{:S(2)}) collective-permute-start(bf16[32,128]{1,0:T(8,128)(2,1)S(1)} %pad_maximum_fusion.4), channel_id=1, source_target_pairs={{0,1},{1,0},{2,3},{3,2},{4,5},{5,4},{6,7},{7,6},{8,9},{9,8},{10,11... | collective-permute-start | bytes 24584 | tf_op jit(solution)/shard_map/ppermute | solution.py:320
  2.3 12.8 %collective-permute-start.5 = (bf16[12,64,128]{2,1,0:T(8,128)(2,1)S(1)}, bf16[12,64,128]{2,1,0:T(8,128)(2,1)S(1)}, u32[]{:S(2)}, u32[]{:S(2)}) collective-permute-start(bf16[12,64,128]{2,1,0:T(8,128)(2,1)S(1)} %pad_maximum_fusion.wz0), channel_id=1, source_target_pairs={{0,24},{8,16},{16,8},{24,0},{1,25},{9,17},{17,9},{25,1},{2,26},{10... | collective-permute-start | bytes 589832 | tf_op jit(solution)/shard_map/ppermute | solution.py:320
  5.8 9.7 %collective-permute-start.4 = (bf16[12,64,128]{2,1,0:T(8,128)(2,1)S(1)}, bf16[12,64,128]{2,1,0:T(8,128)(2,1)S(1)}, u32[]{:S(2)}, u32[]{:S(2)}) collective-permute-start(bf16[12,64,128]{2,1,0:T(8,128)(2,1)S(1)} %pad_maximum_fusion.wz0), channel_id=1, source_target_pairs={{0,16},{8,24},{16,0},{24,8},{1,17},{9,25},{17,1},{25,9},{2,18},{10... | collective-permute-start | bytes 589832 | tf_op jit(solution)/shard_map/ppermute | solution.py:320
  6.3 9.5 %collective-permute-start.3 = (bf16[12,64,128]{2,1,0:T(8,128)(2,1)S(1)}, bf16[12,64,128]{2,1,0:T(8,128)(2,1)S(1)}, u32[]{:S(2)}, u32[]{:S(2)}) collective-permute-start(bf16[12,64,128]{2,1,0:T(8,128)(2,1)S(1)} %pad_maximum_fusion.wz0), channel_id=1, source_target_pairs={{0,8},{8,0},{16,24},{24,16},{1,9},{9,1},{17,25},{25,17},{2,10},{10... | collective-permute-start | bytes 589832 | tf_op jit(solution)/shard_map/ppermute | solution.py:320
  6.4 3.7 %collective-permute-start.1 = (bf16[2,32,128]{2,1,0:T(8,128)(2,1)S(1)}, bf16[2,32,128]{2,1,0:T(8,128)(2,1)S(1)}, u32[]{:S(2)}, u32[]{:S(2)}) collective-permute-start(bf16[2,32,128]{2,1,0:T(8,128)(2,1)S(1)} %pad_maximum_fusion.2), channel_id=1, source_target_pairs={{0,2},{1,3},{2,0},{3,1},{4,6},{5,7},{6,4},{7,5},{8,10},{9,11},{10,... | collective-permute-start | bytes 49160 | tf_op jit(solution)/shard_map/ppermute | solution.py:320
  10.2 4.9 %collective-permute-start.2 = (bf16[4,32,128]{2,1,0:T(8,128)(2,1)S(1)}, bf16[4,32,128]{2,1,0:T(8,128)(2,1)S(1)}, u32[]{:S(2)}, u32[]{:S(2)}) collective-permute-start(bf16[4,32,128]{2,1,0:T(8,128)(2,1)S(1)} %pad_maximum_fusion.1.near), channel_id=1, source_target_pairs={{0,4},{1,5},{2,6},{3,7},{4,0},{5,1},{6,2},{7,3},{8,12},{9,13},{10,... | collective-permute-start | bytes 98312 | tf_op jit(solution)/shard_map/ppermute | solution.py:320

commit v4 on v3

--- a/solution.py
+++ b/solution.py
@@ -75,7 +75,7 @@
     return beside(first, first, pick(64, low, high))
 
 
-def inverse_factors(rows_ref, result_ref, at=0):
+def inverse_factors(rows_ref, result_ref, at=0, beside_it=()):
     sub = lax.broadcasted_iota(jnp.int32, (8, SLOTS), 0)
     one = [(sub == p).astype(F32) for p in range(8)]
     a = []
@@ -90,7 +90,10 @@
     def less(x, m, y):
         return -(m * y) if x is None else x - m * y
 
+    beside_it = list(beside_it)
     for b in range(4):
+        for _ in range(-(-len(beside_it) // (4 - b))):
+            beside_it.pop(0)()
         r, s = a[8 * b : 8 * b + 8], e[8 * b : 8 * b + 8]
         d = [[spread(r[p][b], q) for p in range(q + 1)] for q in range(8)]
         m = [[None] * 8 for _ in range(8)]
@@ -124,7 +127,7 @@
 
 
 def kernel(
-    place, near, far, mask_hbm, start_hbm, wz0, wz1, wz2, wz3, left, right, dense_hbm, out_hbm,
+    place, near, far, first_factors, mask_hbm, start_hbm, wz0, wz1, wz2, wz3, left, right, dense_hbm, out_hbm,
     dense, updated, left_rows, left_columns, right_rows, inner_rows, gram, gram_parts, right_parts, mixer, mixer_parts,
     raw, square, mix_parts, start, basis, imaged, image_parts, wide_rows, rows, factors, mask, load_sem, out_sem,
 ):
@@ -132,8 +135,9 @@
     r, c = place()
     every = range(tiles)
 
-    def drain(t):
-        return pltpu.make_async_copy(updated.at[t], out_hbm.at[t], out_sem.at[t])
+    def drain(t, half):
+        at = pl.ds(half * (order // 2), order // 2)
+        return pltpu.make_async_copy(updated.at[t, at], out_hbm.at[t, at], out_sem.at[t, half])
 
     loads = []
     for q, wz in enumerate((wz0, wz1, wz2, wz3)):
@@ -146,7 +150,7 @@
     loads.append((mask_hbm, mask))
     loads.append((dense_hbm, dense))
     loads = [pltpu.make_async_copy(x, y, load_sem.at[i]) for i, (x, y) in enumerate(loads)]
-    for copy in loads:
+    for copy in loads[:-1]:
         copy.start()
 
     lanes = lax.broadcasted_iota(jnp.int32, (rank, 128), 1)
@@ -163,6 +167,7 @@
         left_rows[t, rank:, :] = outer
     for copy in loads[:-1]:
         copy.wait()
+    loads[-1].start()
 
     row = lax.broadcasted_iota(jnp.int32, (64, 128), 0)
     lane = lax.broadcasted_iota(jnp.int32, (64, 128), 1)
@@ -173,21 +178,16 @@
     for t in every:
         raw[t] = dot(left_rows[t], below(left_rows[t], left_rows[t]), NT)
     for t in every:
-        square[t] = dot(right_rows[t], below(right_rows[t], right_rows[t]), NT) + identity
-    for t in every:
         own = -coupling[t * rank : (t + 1) * rank, :]
         mixer[t] = below(identity[:rank], jnp.where(tail, own, 0.0))
         basis[t] = dot(left_32(own), right_32(raw[t, rank:, :]))
     for t in every:
         mixer_parts[t] = right_64(mixer[t])
-        right_parts[t] = right_64(square[t])
     for t in every:
         scale = wide_right(mixer[t])
         gram[t] = dot(wide_left(below(raw[t, :rank, :], basis[t])), below(scale, scale), NT) + identity
     for t in every:
         gram_parts[t] = right_64(gram[t])
-        wide_rows[pl.ds(t, rank, SLOTS), :] = gram[t, :rank, :]
-        left_columns[t] = jnp.transpose(below(left_rows[t], left_rows[t]))
 
     def inverse(t):
         return factors[pl.ds(t, rank, SLOTS), :]
@@ -196,9 +196,8 @@
     head = left_32(beside(head, head, head, head))
     foot = start[:, rank : 2 * rank]
     foot = left_32(beside(foot, foot, foot, foot))
-    inverse_factors(wide_rows, factors)
-    for t in every:
-        basis[t] = dot(left_32(inverse(t)), right_32(gram[t, :rank, :]))
+    for t in every:
+        basis[t] = dot(left_32(first_factors[pl.ds(t, rank, SLOTS), :]), right_32(gram[t, :rank, :]))
     for t in every:
         mix_parts[t] = right_32(basis[t])
     for t in every:
@@ -206,11 +205,15 @@
         high, middle, low = first[:32], first[32:64], first[128:160]
         square[t] = dot(below(high, high, middle, middle, high, low)[:, :64], first, TN)
     for t in every:
-        imaged[t] = dot(head, mix_parts[t])
-    for t in every:
         basis[t] = jnp.where(tail, gram[t, rank:, :] - square[t, rank:, :], 0.0)
         wide_rows[pl.ds(t, rank, SLOTS), :] = basis[t]
-    inverse_factors(wide_rows, factors, rank)
+
+    def later(t):
+        imaged[t] = dot(head, mix_parts[t])
+        right_parts[t] = right_64(dot(right_rows[t], below(right_rows[t], right_rows[t]), NT) + identity)
+        left_columns[t] = jnp.transpose(below(left_rows[t], left_rows[t]))
+
+    inverse_factors(wide_rows, factors, rank, [functools.partial(later, t) for t in every])
     for t in every:
         basis[t] = dot(left_32(inverse(t)), right_32(basis[t]))
     for t in every:
@@ -256,10 +259,12 @@
         for m in range(0, order, 128):
             added = jnp.where(admissible, 0.0, dense[t, m : m + 128, :].astype(F32))
             updated[t, m : m + 128, :] = (dot(combined[m : m + 128, :], right_rows[t]) + added).astype(BF16)
-        drain(t).start()
+            if m % (order // 2):
+                drain(t, m // (order // 2)).start()
         combined = following
     for t in every:
-        drain(t).wait()
+        drain(t, 0).wait()
+        drain(t, 1).wait()
 
 
 def paired(x):
@@ -267,7 +272,46 @@
     return below(high, low, high)
 
 
-def local_step(place, near, far, mask, start, wzs, left, right, dense):
+def own_grams(left_hbm, result, left, sem):
+    tiles, rank, _ = left.shape
+    copy = pltpu.make_async_copy(left_hbm, left, sem)
+    copy.start()
+    copy.wait()
+    row = lax.broadcasted_iota(jnp.int32, (rank, 128), 0)
+    lane = lax.broadcasted_iota(jnp.int32, (rank, 128), 1)
+    identity = (lane % rank == row).astype(F32)
+    for t in range(tiles):
+        own = left[t]
+        result[pl.ds(t, rank, SLOTS), :] = dot(own, below(own, own, own, own), NT) + identity
+
+
+LIMIT = pltpu.CompilerParams(vmem_limit_bytes=53964 * 1024)
+
+
+def local_grams(left):
+    vmem = pl.BlockSpec(memory_space=pltpu.VMEM)
+    return pl.pallas_call(
+        own_grams,
+        out_shape=jax.ShapeDtypeStruct((32 * SLOTS, 128), F32),
+        in_specs=[pl.BlockSpec(memory_space=pltpu.HBM)],
+        out_specs=vmem,
+        scratch_shapes=[pltpu.VMEM(left.shape, BF16), pltpu.SemaphoreType.DMA],
+        compiler_params=LIMIT,
+    )(left)
+
+
+def local_factors(grams):
+    vmem = pl.BlockSpec(memory_space=pltpu.VMEM)
+    return pl.pallas_call(
+        inverse_factors,
+        out_shape=jax.ShapeDtypeStruct((32 * SLOTS, 128), F32),
+        in_specs=[vmem],
+        out_specs=vmem,
+        compiler_params=LIMIT,
+    )(grams)
+
+
+def local_step(place, near, far, first_factors, mask, start, wzs, left, right, dense):
     tiles, rank, order = left.shape
     vmem = pl.BlockSpec(memory_space=pltpu.VMEM)
     hbm = pl.BlockSpec(memory_space=pltpu.HBM)
@@ -280,7 +324,7 @@
     return pl.pallas_call(
         functools.partial(kernel, place),
         out_shape=jax.ShapeDtypeStruct(dense.shape, BF16),
-        in_specs=[vmem, vmem, free, free] + [free] * 4 + [hbm] * 3,
+        in_specs=[vmem, vmem, vmem, free, free] + [free] * 4 + [hbm] * 3,
         out_specs=hbm,
         scratch_shapes=[
             whole,
@@ -306,10 +350,10 @@
             pltpu.VMEM((32 * SLOTS, 128), F32),
             pltpu.SMEM((1, tiles), jnp.int32),
             pltpu.SemaphoreType.DMA((13,)),
-            pltpu.SemaphoreType.DMA((tiles,)),
+            pltpu.SemaphoreType.DMA((tiles, 2)),
         ],
-        compiler_params=pltpu.CompilerParams(vmem_limit_bytes=53 * 1024 * 1024),
-    )(near, far, mask, start, *wzs, left, right, dense)
+        compiler_params=LIMIT,
+    )(near, far, first_factors, mask, start, *wzs, left, right, dense)
 
 
 def turn(x):
@@ -326,26 +370,33 @@
     def shards(
         panel_outer, panel_inner, upper_inner, upper_outer, tile_left, tile_right, dense_rows, tile_mask, start_block
     ):
-        pair = jnp.concatenate([turn(panel_outer[0]), turn(panel_inner[0])], -1)
-        wz = jnp.concatenate([turn(upper_inner), turn(upper_outer)], 1)
+        left, right = turn(tile_left[0]), turn(tile_right[0])
         if nrow == 4 and ncol == 8:
             place = lambda: (lax.axis_index("row"), lax.axis_index("col"))
+            pair = jnp.concatenate([turn(panel_outer[0]), turn(panel_inner[0])], -1)
+            wz = jnp.concatenate([turn(upper_inner), turn(upper_outer)], 1)
             pair, wz = lax.optimization_barrier((pair, wz))
             near = jnp.stack([pair, swap(pair, "col", 8, 1)])
             wzs = [wz] + [swap(wz, "row", 4, s) for s in (1, 2, 3)]
+            near, left_late = lax.optimization_barrier((near, left))
+            grams = local_grams(left_late)
             near = jnp.concatenate([near, swap(near, "col", 8, 2)])
+            near, grams = lax.optimization_barrier((near, grams))
             far = swap(near, "col", 8, 4)
+            first = local_factors(grams)
         else:
             place = lambda: (0, 0)
+            wz = jnp.concatenate([turn(upper_inner), turn(upper_outer)], 1)
             both = lax.all_gather(jnp.stack([turn(panel_outer[0]), turn(panel_inner[0])]), "col", axis=2, tiled=True)
             xy = jnp.concatenate([both[0].reshape(32, 8, 64), both[1].reshape(32, 8, 64)], -1).swapaxes(0, 1)
             near, far = xy[:4], xy[4:]
             wz = lax.all_gather(wz, "row", axis=2, tiled=True)
             wzs = [wz[:, :, 128 * q : 128 * q + 128] for q in range(4)]
+            first = local_factors(local_grams(left))
         flags = (tile_mask == 1).astype(jnp.int32)
         start = jnp.concatenate([turn(start_block), turn(start_block)], 1)
         updated = local_step(
-            place, near, far, flags, start, wzs, turn(tile_left[0]), turn(tile_right[0]), dense_rows[0]
+            place, near, far, first, flags, start, wzs, left, right, dense_rows[0]
         )
         return updated[None]
 

time: 31.4 us -> 29.7 us (0.946)
  waiting for transfers between devices: 2.87 us -> 0.53 us
  local copies, waits for them, and re-layouts: 0 us -> 1 us
  starting transfers between devices: 9.64 us -> 9.31 us
    ppermute x6, waiting for transfers between devices: 2.87 us -> 0.53 us  [swap(): return lax.ppermute(x, axis, [(i, i ^ step) for i in range(size)])]
    pallas_call x0 -> x2, Pallas kernels: none -> 1.67 us  [the longest x1 0.84 us: local_factors(): pl.pallas_call(inverse_factors, out_shape=jax.ShapeDtypeStruct((32 * SLOT...]
    pallas_call x1, Pallas kernels: 15.1 us -> 13.4 us  [local_step(): pl.pallas_call(functools.partial(kernel, place), out_shape=jax.ShapeDtype...]
    unnamed x0 -> x2, local copies, waits for them, and re-layouts: none -> 1 us
    ppermute x6, starting transfers between devices: 9.64 us -> 9.31 us  [swap(): return lax.ppermute(x, axis, [(i, i ^ step) for i in range(size)])]
  transfers between devices with their start and end apart: 6 -> 6, of which waited for: 4 -> 1; matrix products, arithmetic and copies ran while one was open for 5% -> 5% of each run, Pallas kernels for 0% -> 6%
where the time goes in v4:
time: 29.7 us; the launch traced here: 29.3 us
  Pallas kernels  15.1 us (51%)
  starting transfers between devices  9.31 us (31%)
  other arithmetic  3.28 us (11%)
  local copies, waits for them, and re-layouts  1 us (3%)
  waiting for transfers between devices  0.53 us (2%)
    pallas_call x1, Pallas kernels, local_step(): pl.pallas_call(functools.partial(kernel, place), out_shape=jax.ShapeDtype...  13.4 us
    ppermute x6, starting transfers between devices, swap(): return lax.ppermute(x, axis, [(i, i ^ step) for i in range(size)])  9.31 us
    unnamed x2, local copies, waits for them, and re-layouts  1 us
    concatenate x1, other arithmetic, shards(): wz = jnp.concatenate([turn(upper_inner), turn(upper_outer)], 1)  0.96 us
    concatenate x1, other arithmetic, shards(): start = jnp.concatenate([turn(start_block), turn(start_block)], 1)  0.87 us
    pallas_call x1, Pallas kernels, local_factors(): pl.pallas_call(inverse_factors, out_shape=jax.ShapeDtypeStruct((32 * SLOT...  0.84 us
    pallas_call x1, Pallas kernels, local_grams(): pl.pallas_call(own_grams, out_shape=jax.ShapeDtypeStruct((32 * SLOTS, 128...  0.82 us
    concatenate x1, other arithmetic, shards(): pair = jnp.concatenate([turn(panel_outer[0]), turn(panel_inner[0])], -1)  0.79 us
  transfers between devices with their start and end apart: 6, of which 1 were waited for; matrix products, arithmetic and copies ran while one was open for 5% of the time, Pallas kernels for 6%

profile of v4, /device:TPU:0, one launch (start us, length us, event | category | flops | bytes accessed | tf_op | source)
XLA Modules:
  0.0 29.3 jit_solution(18410451517951968379)
XLA Ops:
  0.0 0.8 %pad_maximum_fusion.4 = bf16[32,128]{1,0:T(8,128)(2,1)S(1)} fusion(bf16[32,64]{1,0:T(8,128)(2,1)} %bitcast.27, bf16[32,64]{1,0:T(8,128)(2,1)} %bitcast.28), kind=kLoop, calls=%fused_computation.4 | loop fusion | flops 16384 | bytes 16384 | tf_op jit(solution)/shard_map/concatenate | solution.py:376
  0.8 1.0 %pad_maximum_fusion.wz0 = bf16[12,64,128]{2,1,0:T(8,128)(2,1)S(1)} fusion(bf16[12,32,128]{2,1,0:T(8,128)(2,1)} %bitcast.23, bf16[12,32,128]{2,1,0:T(8,128)(2,1)} %bitcast.24), kind=kLoop, calls=%fused_computation | loop fusion | flops 393216 | bytes 393216 | tf_op jit(solution)/shard_map/concatenate | solution.py:377
  1.8 0.5 %collective-permute-start = (bf16[32,128]{1,0:T(8,128)(2,1)S(1)}, bf16[32,128]{1,0:T(8,128)(2,1)S(1)}, u32[]{:S(2)}, u32[]{:S(2)}) collective-permute-start(bf16[32,128]{1,0:T(8,128)(2,1)S(1)} %pad_maximum_fusion.4), channel_id=1, source_target_pairs={{0,1},{1,0},{2,3},{3,2},{4,5},{5,4},{6,7},{7,6},{8,9},{9,8},{10,11... | collective-permute-start | bytes 24584 | tf_op jit(solution)/shard_map/ppermute | solution.py:364
  2.3 3.5 %collective-permute-start.5 = (bf16[12,64,128]{2,1,0:T(8,128)(2,1)S(1)}, bf16[12,64,128]{2,1,0:T(8,128)(2,1)S(1)}, u32[]{:S(2)}, u32[]{:S(2)}) collective-permute-start(bf16[12,64,128]{2,1,0:T(8,128)(2,1)S(1)} %pad_maximum_fusion.wz0), channel_id=1, source_target_pairs={{0,24},{8,16},{16,8},{24,0},{1,25},{9,17},{17,9},{25,1},{2,26},{10... | collective-permute-start | bytes 589832 | tf_op jit(solution)/shard_map/ppermute | solution.py:364
  5.8 0.5 %collective-permute-start.4 = (bf16[12,64,128]{2,1,0:T(8,128)(2,1)S(1)}, bf16[12,64,128]{2,1,0:T(8,128)(2,1)S(1)}, u32[]{:S(2)}, u32[]{:S(2)}) collective-permute-start(bf16[12,64,128]{2,1,0:T(8,128)(2,1)S(1)} %pad_maximum_fusion.wz0), channel_id=1, source_target_pairs={{0,16},{8,24},{16,0},{24,8},{1,17},{9,25},{17,1},{25,9},{2,18},{10... | collective-permute-start | bytes 589832 | tf_op jit(solution)/shard_map/ppermute | solution.py:364
  6.3 0.1 collective-permute-start.3
  6.4 0.0 collective-permute-done
  6.4 2.0 %collective-permute-start.1 = (bf16[2,32,128]{2,1,0:T(8,128)(2,1)S(1)}, bf16[2,32,128]{2,1,0:T(8,128)(2,1)S(1)}, u32[]{:S(2)}, u32[]{:S(2)}) collective-permute-start(bf16[2,32,128]{2,1,0:T(8,128)(2,1)S(1)} %pad_maximum_fusion.2), channel_id=1, source_target_pairs={{0,2},{1,3},{2,0},{3,1},{4,6},{5,7},{6,4},{7,5},{8,10},{9,11},{10,... | collective-permute-start | bytes 49160 | tf_op jit(solution)/shard_map/ppermute | solution.py:364
  8.4 0.7 %compare_convert_fusion.mask_hbm = s32[1,12]{1,0:T(1,128)S(1)} fusion(s32[1,12]{1,0:T(1,128)} %param.16), kind=kLoop, calls=%fused_computation.5 | loop fusion | flops 24 | bytes 96 | tf_op jit(solution)/shard_map/convert_element_type | solution.py:396
  9.1 0.0 copy-start
  9.1 1.0 %copy-done = bf16[1,12,512,32]{2,3,1,0:T(8,128)(2,1)S(1)} copy-done((bf16[1,12,512,32]{2,3,1,0:T(8,128)(2,1)S(1)}, bf16[1,12,512,32]{2,3,1,0:T(8,128)(2,1)}, u32[]{:S(2)}) %copy-start) | copy-done | bytes 393240
  10.1 0.8 %shard_map.91.rows_ref = f32[512,128]{1,0:T(8,128)S(1)} custom-call(bf16[12,32,512]{2,1,0:T(8,128)(2,1)S(1)} %bitcast.20), custom_call_target="tpu_custom_call" | custom-call | tf_op jit(solution)/shard_map/pallas_call | solution.py:293
  10.9 0.0 collective-permute-done.1
  10.9 2.7 %collective-permute-start.2 = (bf16[4,32,128]{2,1,0:T(8,128)(2,1)S(1)}, bf16[4,32,128]{2,1,0:T(8,128)(2,1)S(1)}, u32[]{:S(2)}, u32[]{:S(2)}) collective-permute-start(bf16[4,32,128]{2,1,0:T(8,128)(2,1)S(1)} %pad_maximum_fusion.1.near), channel_id=1, source_target_pairs={{0,4},{1,5},{2,6},{3,7},{4,0},{5,1},{6,2},{7,3},{8,12},{9,13},{10,... | collective-permute-start | bytes 98312 | tf_op jit(solution)/shard_map/ppermute | solution.py:364
  13.6 0.9 %pad_maximum_fusion.3.start_hbm = f32[32,128]{1,0:T(8,128)S(1)} fusion(f32[32,64]{1,0:T(8,128)} %bitcast.26), kind=kLoop, calls=%fused_computation.3 | loop fusion | flops 4096 | bytes 24576 | tf_op jit(solution)/shard_map/concatenate | solution.py:397
  14.4 0.8 %shard_map.92.first_factors = f32[512,128]{1,0:T(8,128)S(1)} custom-call(f32[512,128]{1,0:T(8,128)S(1)} %shard_map.91.rows_ref), custom_call_target="tpu_custom_call" | custom-call | tf_op jit(solution)/shard_map/pallas_call | solution.py:305
  15.3 0.5 %collective-permute-done.2.far = bf16[4,32,128]{2,1,0:T(8,128)(2,1)S(1)} collective-permute-done((bf16[4,32,128]{2,1,0:T(8,128)(2,1)S(1)}, bf16[4,32,128]{2,1,0:T(8,128)(2,1)S(1)}, u32[]{:S(2)}, u32[]{:S(2)}) %collective-permute-start.2) | collective-permute-done | bytes 32800 | tf_op jit(solution)/shard_map/ppermute | solution.py:364
  15.8 0.0 collective-permute-done.5.wz3
  15.8 0.0 collective-permute-done.4.wz2
  15.8 0.0 collective-permute-done.3.wz1
  15.8 13.4 %shard_map.93 = bf16[12,512,512]{2,1,0:T(8,128)(2,1)} custom-call(bf16[4,32,128]{2,1,0:T(8,128)(2,1)S(1)} %pad_maximum_fusion.1.near, bf16[4,32,128]{2,1,0:T(8,128)(2,1)S(1)} %collective-permute-done.2.far, f32[512,128]{1,0:T(8,128)S(1)} %shard_map.92.first_factors, s32[1,12]{1,0:T(1,128)S(1)} %compare_convert_fusion.mask_hbm, ...), custom_call_target="tpu_custom_call" | custom-call | tf_op jit(solution)/shard_map/pallas_call | solution.py:324
  (2 shorter events, 0.0 us)
Async XLA Ops:
  1.8 4.7 %collective-permute-start = (bf16[32,128]{1,0:T(8,128)(2,1)S(1)}, bf16[32,128]{1,0:T(8,128)(2,1)S(1)}, u32[]{:S(2)}, u32[]{:S(2)}) collective-permute-start(bf16[32,128]{1,0:T(8,128)(2,1)S(1)} %pad_maximum_fusion.4), channel_id=1, source_target_pairs={{0,1},{1,0},{2,3},{3,2},{4,5},{5,4},{6,7},{7,6},{8,9},{9,8},{10,11... | collective-permute-start | bytes 24584 | tf_op jit(solution)/shard_map/ppermute | solution.py:364
  2.3 13.5 %collective-permute-start.5 = (bf16[12,64,128]{2,1,0:T(8,128)(2,1)S(1)}, bf16[12,64,128]{2,1,0:T(8,128)(2,1)S(1)}, u32[]{:S(2)}, u32[]{:S(2)}) collective-permute-start(bf16[12,64,128]{2,1,0:T(8,128)(2,1)S(1)} %pad_maximum_fusion.wz0), channel_id=1, source_target_pairs={{0,24},{8,16},{16,8},{24,0},{1,25},{9,17},{17,9},{25,1},{2,26},{10... | collective-permute-start | bytes 589832 | tf_op jit(solution)/shard_map/ppermute | solution.py:364
  5.8 10.0 %collective-permute-start.4 = (bf16[12,64,128]{2,1,0:T(8,128)(2,1)S(1)}, bf16[12,64,128]{2,1,0:T(8,128)(2,1)S(1)}, u32[]{:S(2)}, u32[]{:S(2)}) collective-permute-start(bf16[12,64,128]{2,1,0:T(8,128)(2,1)S(1)} %pad_maximum_fusion.wz0), channel_id=1, source_target_pairs={{0,16},{8,24},{16,0},{24,8},{1,17},{9,25},{17,1},{25,9},{2,18},{10... | collective-permute-start | bytes 589832 | tf_op jit(solution)/shard_map/ppermute | solution.py:364
  6.3 9.5 %collective-permute-start.3 = (bf16[12,64,128]{2,1,0:T(8,128)(2,1)S(1)}, bf16[12,64,128]{2,1,0:T(8,128)(2,1)S(1)}, u32[]{:S(2)}, u32[]{:S(2)}) collective-permute-start(bf16[12,64,128]{2,1,0:T(8,128)(2,1)S(1)} %pad_maximum_fusion.wz0), channel_id=1, source_target_pairs={{0,8},{8,0},{16,24},{24,16},{1,9},{9,1},{17,25},{25,17},{2,10},{10... | collective-permute-start | bytes 589832 | tf_op jit(solution)/shard_map/ppermute | solution.py:364
  6.4 4.5 %collective-permute-start.1 = (bf16[2,32,128]{2,1,0:T(8,128)(2,1)S(1)}, bf16[2,32,128]{2,1,0:T(8,128)(2,1)S(1)}, u32[]{:S(2)}, u32[]{:S(2)}) collective-permute-start(bf16[2,32,128]{2,1,0:T(8,128)(2,1)S(1)} %pad_maximum_fusion.2), channel_id=1, source_target_pairs={{0,2},{1,3},{2,0},{3,1},{4,6},{5,7},{6,4},{7,5},{8,10},{9,11},{10,... | collective-permute-start | bytes 49160 | tf_op jit(solution)/shard_map/ppermute | solution.py:364
  9.1 1.0 %copy-start = (bf16[1,12,512,32]{2,3,1,0:T(8,128)(2,1)S(1)}, bf16[1,12,512,32]{2,3,1,0:T(8,128)(2,1)}, u32[]{:S(2)}) copy-start(bf16[1,12,512,32]{2,3,1,0:T(8,128)(2,1)} %param.13) | copy-start | bytes 1179652
  10.9 4.9 %collective-permute-start.2 = (bf16[4,32,128]{2,1,0:T(8,128)(2,1)S(1)}, bf16[4,32,128]{2,1,0:T(8,128)(2,1)S(1)}, u32[]{:S(2)}, u32[]{:S(2)}) collective-permute-start(bf16[4,32,128]{2,1,0:T(8,128)(2,1)S(1)} %pad_maximum_fusion.1.near), channel_id=1, source_target_pairs={{0,4},{1,5},{2,6},{3,7},{4,0},{5,1},{6,2},{7,3},{8,12},{9,13},{10,... | collective-permute-start | bytes 98312 | tf_op jit(solution)/shard_map/ppermute | solution.py:364

commit v5 on v4

--- a/solution.py
+++ b/solution.py
@@ -127,9 +127,9 @@
 
 
 def kernel(
-    place, near, far, first_factors, mask_hbm, start_hbm, wz0, wz1, wz2, wz3, left, right, dense_hbm, out_hbm,
-    dense, updated, left_rows, left_columns, right_rows, inner_rows, gram, gram_parts, right_parts, mixer, mixer_parts,
-    raw, square, mix_parts, start, basis, imaged, image_parts, wide_rows, rows, factors, mask, load_sem, out_sem,
+    place, near, far, first_factors, flags, start, wz0, wz1, wz2, wz3, left, right, dense_hbm, out_hbm,
+    dense, updated, left_rows, left_columns, right_rows, gram, gram_parts, right_parts, mixer, mixer_parts,
+    raw, square, mix_parts, basis, imaged, image_parts, wide_rows, rows, factors, mask, load_sem, out_sem,
 ):
     tiles, rank, order = left.shape
     r, c = place()
@@ -139,42 +139,41 @@
         at = pl.ds(half * (order // 2), order // 2)
         return pltpu.make_async_copy(updated.at[t, at], out_hbm.at[t, at], out_sem.at[t, half])
 
-    loads = []
+    loads = [(left, left_rows.at[:, :rank, :]), (right, right_rows.at[:, :rank, :]), (flags, mask)]
     for q, wz in enumerate((wz0, wz1, wz2, wz3)):
         at = pl.ds(pl.multiple_of((r ^ q) * 128, 128), 128)
-        loads.append((wz.at[:, :rank, :], inner_rows.at[:, :, at]))
         loads.append((wz.at[:, rank:, :], right_rows.at[:, rank:, at]))
-    loads.append((left, left_rows.at[:, :rank, :]))
-    loads.append((right, right_rows.at[:, :rank, :]))
-    loads.append((start_hbm, start))
-    loads.append((mask_hbm, mask))
     loads.append((dense_hbm, dense))
     loads = [pltpu.make_async_copy(x, y, load_sem.at[i]) for i, (x, y) in enumerate(loads)]
     for copy in loads[:-1]:
         copy.start()
 
     lanes = lax.broadcasted_iota(jnp.int32, (rank, 128), 1)
-    outer, inner = [], []
+
+    def blocks(q):
+        found = []
+        for p in (c ^ (2 * q), c ^ (2 * q + 1)):
+            found.append(jnp.where(p < 4, near[p % 4].astype(F32), far[p % 4].astype(F32)))
+        return found
+
+    coupling = 0.0
+    for q, wz in enumerate((wz0, wz1, wz2, wz3)):
+        even, odd = blocks(r ^ q)
+        inner = jnp.where(lanes < 64, pltpu.roll(even, 64, 1), odd).astype(BF16)
+        coupling += dot(wz[:, :rank, :].reshape(tiles * rank, 128), below(inner, inner, inner, inner), NT)
+    outer = []
     for q in range(4):
-        even, odd = [
-            jnp.where((c ^ p) < 4, near[(c ^ p) % 4].astype(F32), far[(c ^ p) % 4].astype(F32)) for p in (2 * q, 2 * q + 1)
-        ]
+        even, odd = blocks(q)
         outer.append(jnp.where(lanes < 64, even, pltpu.roll(odd, 64, 1)).astype(BF16))
-        inner.append(jnp.where(lanes < 64, pltpu.roll(even, 64, 1), odd).astype(BF16))
     outer = beside(*outer)
-    inner = beside(*inner)
     for t in every:
         left_rows[t, rank:, :] = outer
-    for copy in loads[:-1]:
-        copy.wait()
-    loads[-1].start()
-
+    loads[0].wait()
     row = lax.broadcasted_iota(jnp.int32, (64, 128), 0)
     lane = lax.broadcasted_iota(jnp.int32, (64, 128), 1)
     identity = (lane % 64 == row).astype(F32)
     tail = lane[:rank] % 64 >= rank
 
-    coupling = dot(inner_rows[...].reshape(tiles * rank, order), below(inner, inner, inner, inner), NT)
     for t in every:
         raw[t] = dot(left_rows[t], below(left_rows[t], left_rows[t]), NT)
     for t in every:
@@ -188,6 +187,10 @@
         gram[t] = dot(wide_left(below(raw[t, :rank, :], basis[t])), below(scale, scale), NT) + identity
     for t in every:
         gram_parts[t] = right_64(gram[t])
+
+    for copy in loads[1:-1]:
+        copy.wait()
+    loads[-1].start()
 
     def inverse(t):
         return factors[pl.ds(t, rank, SLOTS), :]
@@ -224,27 +227,32 @@
         for t in every:
             imaged[t] = dot(left_64(basis[t]), gram_parts[t])
         for t in every:
-            image_parts[t] = below(*parts3(imaged[t]))
-            rows[pl.ds(t, rank, SLOTS), :] = dot(wide_left(imaged[t]), wide_right(basis[t]), NT)
-        inverse_factors(rows, factors)
+            high, middle, low = parts3(imaged[t])
+            image_parts[t] = below(high, middle, low)
+            rows[pl.ds(t, rank, SLOTS), :] = dot(
+                beside(high, middle, pick(64, high, low)), wide_right(basis[t]), NT
+            )
         if step < ITERS - 1:
+            inverse_factors(rows, factors)
             for t in every:
                 imaged[t] = dot(inverse(t).astype(BF16)[:, :96], image_parts[t])
-        else:
-            for t in every:
-                scale = pick(64, *parts2(inverse(t)))
-                high, middle = image_parts[t, :32, :], image_parts[t, 32:64, :]
-                imaged[t] = dot(scale, below(high, middle, high, middle))
-                high, middle = parts2(basis[t])
-                basis[t] = dot(scale, below(high, middle, high, middle))
+
+    def spread(t):
+        basis[t] = dot(left_64(basis[t]), mixer_parts[t])
+
+    inverse_factors(rows, factors, 0, [functools.partial(spread, t) for t in every])
+    for t in every:
+        scale = pick(64, *parts2(inverse(t)))
+        high, middle = image_parts[t, :32, :], image_parts[t, 32:64, :]
+        imaged[t] = dot(scale, below(high, middle, high, middle))
+        high, middle = parts2(basis[t])
+        basis[t] = dot(scale, below(high, middle, high, middle))
 
     loads[-1].wait()
     last = (lane[:rank] % 64 == row[:rank] + rank).astype(F32)
     for t in every:
-        square[t, :rank, :] = dot(left_64(basis[t]), mixer_parts[t])
-    for t in every:
         admissible = mask[0, t] == 1
-        high, low = parts2(jnp.where(admissible, square[t, :rank, :], mixer[t, rank:, :])[:, :64])
+        high, low = parts2(jnp.where(admissible, basis[t], mixer[t, rank:, :])[:, :64])
         raw[t] = dot(below(high, high, low), paired(jnp.where(admissible, imaged[t], last)), TN)
     for t in every:
         mix_parts[t, :128, :] = below(*parts2(raw[t]))
@@ -272,11 +280,8 @@
     return below(high, low, high)
 
 
-def own_grams(left_hbm, result, left, sem):
+def own_grams(left, result):
     tiles, rank, _ = left.shape
-    copy = pltpu.make_async_copy(left_hbm, left, sem)
-    copy.start()
-    copy.wait()
     row = lax.broadcasted_iota(jnp.int32, (rank, 128), 0)
     lane = lax.broadcasted_iota(jnp.int32, (rank, 128), 1)
     identity = (lane % rank == row).astype(F32)
@@ -285,7 +290,7 @@
         result[pl.ds(t, rank, SLOTS), :] = dot(own, below(own, own, own, own), NT) + identity
 
 
-LIMIT = pltpu.CompilerParams(vmem_limit_bytes=53964 * 1024)
+LIMIT = pltpu.CompilerParams(vmem_limit_bytes=54000 * 1024)
 
 
 def local_grams(left):
@@ -293,9 +298,8 @@
     return pl.pallas_call(
         own_grams,
         out_shape=jax.ShapeDtypeStruct((32 * SLOTS, 128), F32),
-        in_specs=[pl.BlockSpec(memory_space=pltpu.HBM)],
+        in_specs=[vmem],
         out_specs=vmem,
-        scratch_shapes=[pltpu.VMEM(left.shape, BF16), pltpu.SemaphoreType.DMA],
         compiler_params=LIMIT,
     )(left)
 
@@ -311,7 +315,7 @@
     )(grams)
 
 
-def local_step(place, near, far, first_factors, mask, start, wzs, left, right, dense):
+def local_step(place, near, far, first_factors, flags, start, wzs, left, right, dense):
     tiles, rank, order = left.shape
     vmem = pl.BlockSpec(memory_space=pltpu.VMEM)
     hbm = pl.BlockSpec(memory_space=pltpu.HBM)
@@ -324,7 +328,7 @@
     return pl.pallas_call(
         functools.partial(kernel, place),
         out_shape=jax.ShapeDtypeStruct(dense.shape, BF16),
-        in_specs=[vmem, vmem, vmem, free, free] + [free] * 4 + [hbm] * 3,
+        in_specs=[vmem] * 3 + [free] + [vmem] * 5 + [hbm] * 3,
         out_specs=hbm,
         scratch_shapes=[
             whole,
@@ -332,7 +336,6 @@
             rows,
             pltpu.VMEM((tiles, order, 128), BF16),
             rows,
-            pltpu.VMEM((tiles, rank, order), BF16),
             square,
             parts,
             parts,
@@ -341,7 +344,6 @@
             square,
             square,
             parts,
-            pltpu.VMEM((32, 128), F32),
             small,
             small,
             pltpu.VMEM((tiles, 96, 128), BF16),
@@ -349,11 +351,11 @@
             pltpu.VMEM((32 * SLOTS, 32), F32),
             pltpu.VMEM((32 * SLOTS, 128), F32),
             pltpu.SMEM((1, tiles), jnp.int32),
-            pltpu.SemaphoreType.DMA((13,)),
+            pltpu.SemaphoreType.DMA((8,)),
             pltpu.SemaphoreType.DMA((tiles, 2)),
         ],
         compiler_params=LIMIT,
-    )(near, far, first_factors, mask, start, *wzs, left, right, dense)
+    )(near, far, first_factors, flags, start, *wzs, left, right, dense)
 
 
 def turn(x):

time: 29.7 us -> 29.4 us (0.990)
  Pallas kernels: 15.1 us -> 14.7 us
  transfers between devices with their start and end apart: 6 -> 6, of which waited for: 1 -> 2; matrix products, arithmetic and copies ran while one was open for 5% -> 5% of each run, Pallas kernels for 6% -> 5%
where the time goes in v5:
time: 29.4 us; the launch traced here: 29 us
  Pallas kernels  14.7 us (50%)
  starting transfers between devices  9.31 us (32%)
  other arithmetic  3.28 us (11%)
  local copies, waits for them, and re-layouts  1 us (3%)
  waiting for transfers between devices  0.72 us (2%)
    pallas_call x1, Pallas kernels, local_step(): pl.pallas_call(functools.partial(kernel, place), out_shape=jax.ShapeDtype...  13.2 us
    ppermute x6, starting transfers between devices, swap(): return lax.ppermute(x, axis, [(i, i ^ step) for i in range(size)])  9.31 us
    unnamed x2, local copies, waits for them, and re-layouts  1 us
    concatenate x1, other arithmetic, shards(): wz = jnp.concatenate([turn(upper_inner), turn(upper_outer)], 1)  0.96 us
    concatenate x1, other arithmetic, shards(): start = jnp.concatenate([turn(start_block), turn(start_block)], 1)  0.87 us
    pallas_call x1, Pallas kernels, local_factors(): pl.pallas_call(inverse_factors, out_shape=jax.ShapeDtypeStruct((32 * SLOT...  0.84 us
    concatenate x1, other arithmetic, shards(): pair = jnp.concatenate([turn(panel_outer[0]), turn(panel_inner[0])], -1)  0.79 us
    ppermute x6, waiting for transfers between devices, swap(): return lax.ppermute(x, axis, [(i, i ^ step) for i in range(size)])  0.72 us
  transfers between devices with their start and end apart: 6, of which 2 were waited for; matrix products, arithmetic and copies ran while one was open for 5% of the time, Pallas kernels for 5%

profile of v5, /device:TPU:0, one launch (start us, length us, event | category | flops | bytes accessed | tf_op | source)
XLA Modules:
  0.0 29.0 jit_solution(18288698279566559504)
XLA Ops:
  0.0 0.8 %pad_maximum_fusion.4 = bf16[32,128]{1,0:T(8,128)(2,1)S(1)} fusion(bf16[32,64]{1,0:T(8,128)(2,1)} %bitcast.27, bf16[32,64]{1,0:T(8,128)(2,1)} %bitcast.28), kind=kLoop, calls=%fused_computation.4 | loop fusion | flops 16384 | bytes 16384 | tf_op jit(solution)/shard_map/concatenate | solution.py:378
  0.8 1.0 %pad_maximum_fusion.wz0 = bf16[12,64,128]{2,1,0:T(8,128)(2,1)S(1)} fusion(bf16[12,32,128]{2,1,0:T(8,128)(2,1)} %bitcast.23, bf16[12,32,128]{2,1,0:T(8,128)(2,1)} %bitcast.24), kind=kLoop, calls=%fused_computation | loop fusion | flops 393216 | bytes 393216 | tf_op jit(solution)/shard_map/concatenate | solution.py:379
  1.8 0.5 %collective-permute-start = (bf16[32,128]{1,0:T(8,128)(2,1)S(1)}, bf16[32,128]{1,0:T(8,128)(2,1)S(1)}, u32[]{:S(2)}, u32[]{:S(2)}) collective-permute-start(bf16[32,128]{1,0:T(8,128)(2,1)S(1)} %pad_maximum_fusion.4), channel_id=1, source_target_pairs={{0,1},{1,0},{2,3},{3,2},{4,5},{5,4},{6,7},{7,6},{8,9},{9,8},{10,11... | collective-permute-start | bytes 24584 | tf_op jit(solution)/shard_map/ppermute | solution.py:366
  2.3 3.5 %collective-permute-start.5 = (bf16[12,64,128]{2,1,0:T(8,128)(2,1)S(1)}, bf16[12,64,128]{2,1,0:T(8,128)(2,1)S(1)}, u32[]{:S(2)}, u32[]{:S(2)}) collective-permute-start(bf16[12,64,128]{2,1,0:T(8,128)(2,1)S(1)} %pad_maximum_fusion.wz0), channel_id=1, source_target_pairs={{0,24},{8,16},{16,8},{24,0},{1,25},{9,17},{17,9},{25,1},{2,26},{10... | collective-permute-start | bytes 589832 | tf_op jit(solution)/shard_map/ppermute | solution.py:366
  5.8 0.5 %collective-permute-start.4 = (bf16[12,64,128]{2,1,0:T(8,128)(2,1)S(1)}, bf16[12,64,128]{2,1,0:T(8,128)(2,1)S(1)}, u32[]{:S(2)}, u32[]{:S(2)}) collective-permute-start(bf16[12,64,128]{2,1,0:T(8,128)(2,1)S(1)} %pad_maximum_fusion.wz0), channel_id=1, source_target_pairs={{0,16},{8,24},{16,0},{24,8},{1,17},{9,25},{17,1},{25,9},{2,18},{10... | collective-permute-start | bytes 589832 | tf_op jit(solution)/shard_map/ppermute | solution.py:366
  6.3 0.1 collective-permute-start.3
  6.4 0.0 collective-permute-done
  6.4 2.0 %collective-permute-start.1 = (bf16[2,32,128]{2,1,0:T(8,128)(2,1)S(1)}, bf16[2,32,128]{2,1,0:T(8,128)(2,1)S(1)}, u32[]{:S(2)}, u32[]{:S(2)}) collective-permute-start(bf16[2,32,128]{2,1,0:T(8,128)(2,1)S(1)} %pad_maximum_fusion.2), channel_id=1, source_target_pairs={{0,2},{1,3},{2,0},{3,1},{4,6},{5,7},{6,4},{7,5},{8,10},{9,11},{10,... | collective-permute-start | bytes 49160 | tf_op jit(solution)/shard_map/ppermute | solution.py:366
  8.4 0.7 %compare_convert_fusion.flags = s32[1,12]{1,0:T(1,128)S(1)} fusion(s32[1,12]{1,0:T(1,128)} %param.16), kind=kLoop, calls=%fused_computation.5 | loop fusion | flops 24 | bytes 96 | tf_op jit(solution)/shard_map/convert_element_type | solution.py:398
  9.1 0.0 copy-start
  9.1 1.0 %copy-done = bf16[1,12,512,32]{2,3,1,0:T(8,128)(2,1)S(1)} copy-done((bf16[1,12,512,32]{2,3,1,0:T(8,128)(2,1)S(1)}, bf16[1,12,512,32]{2,3,1,0:T(8,128)(2,1)}, u32[]{:S(2)}) %copy-start) | copy-done | bytes 393240
  10.1 0.6 %shard_map.91.rows_ref = f32[512,128]{1,0:T(8,128)S(1)} custom-call(bf16[12,32,512]{2,1,0:T(8,128)(2,1)S(1)} %bitcast.20), custom_call_target="tpu_custom_call" | custom-call | tf_op jit(solution)/shard_map/pallas_call | solution.py:298
  10.7 0.0 collective-permute-done.1
  10.7 2.7 %collective-permute-start.2 = (bf16[4,32,128]{2,1,0:T(8,128)(2,1)S(1)}, bf16[4,32,128]{2,1,0:T(8,128)(2,1)S(1)}, u32[]{:S(2)}, u32[]{:S(2)}) collective-permute-start(bf16[4,32,128]{2,1,0:T(8,128)(2,1)S(1)} %pad_maximum_fusion.1.near), channel_id=1, source_target_pairs={{0,4},{1,5},{2,6},{3,7},{4,0},{5,1},{6,2},{7,3},{8,12},{9,13},{10,... | collective-permute-start | bytes 98312 | tf_op jit(solution)/shard_map/ppermute | solution.py:366
  13.4 0.9 %pad_maximum_fusion.3.start = f32[32,128]{1,0:T(8,128)S(1)} fusion(f32[32,64]{1,0:T(8,128)} %bitcast.26), kind=kLoop, calls=%fused_computation.3 | loop fusion | flops 4096 | bytes 24576 | tf_op jit(solution)/shard_map/concatenate | solution.py:399
  14.3 0.8 %shard_map.92.first_factors = f32[512,128]{1,0:T(8,128)S(1)} custom-call(f32[512,128]{1,0:T(8,128)S(1)} %shard_map.91.rows_ref), custom_call_target="tpu_custom_call" | custom-call | tf_op jit(solution)/shard_map/pallas_call | solution.py:309
  15.1 0.5 %collective-permute-done.2.far = bf16[4,32,128]{2,1,0:T(8,128)(2,1)S(1)} collective-permute-done((bf16[4,32,128]{2,1,0:T(8,128)(2,1)S(1)}, bf16[4,32,128]{2,1,0:T(8,128)(2,1)S(1)}, u32[]{:S(2)}, u32[]{:S(2)}) %collective-permute-start.2) | collective-permute-done | bytes 32800 | tf_op jit(solution)/shard_map/ppermute | solution.py:366
  15.6 0.0 collective-permute-done.5.wz3
  15.6 0.0 collective-permute-done.4.wz2
  15.6 0.2 collective-permute-done.3.wz1
  15.8 13.2 %shard_map.93 = bf16[12,512,512]{2,1,0:T(8,128)(2,1)} custom-call(bf16[4,32,128]{2,1,0:T(8,128)(2,1)S(1)} %pad_maximum_fusion.1.near, bf16[4,32,128]{2,1,0:T(8,128)(2,1)S(1)} %collective-permute-done.2.far, f32[512,128]{1,0:T(8,128)S(1)} %shard_map.92.first_factors, s32[1,12]{1,0:T(1,128)S(1)} %compare_convert_fusion.flags, ...), custom_call_target="tpu_custom_call" | custom-call | tf_op jit(solution)/shard_map/pallas_call | solution.py:328
  (2 shorter events, 0.0 us)
Async XLA Ops:
  1.8 4.7 %collective-permute-start = (bf16[32,128]{1,0:T(8,128)(2,1)S(1)}, bf16[32,128]{1,0:T(8,128)(2,1)S(1)}, u32[]{:S(2)}, u32[]{:S(2)}) collective-permute-start(bf16[32,128]{1,0:T(8,128)(2,1)S(1)} %pad_maximum_fusion.4), channel_id=1, source_target_pairs={{0,1},{1,0},{2,3},{3,2},{4,5},{5,4},{6,7},{7,6},{8,9},{9,8},{10,11... | collective-permute-start | bytes 24584 | tf_op jit(solution)/shard_map/ppermute | solution.py:366
  2.3 13.3 %collective-permute-start.5 = (bf16[12,64,128]{2,1,0:T(8,128)(2,1)S(1)}, bf16[12,64,128]{2,1,0:T(8,128)(2,1)S(1)}, u32[]{:S(2)}, u32[]{:S(2)}) collective-permute-start(bf16[12,64,128]{2,1,0:T(8,128)(2,1)S(1)} %pad_maximum_fusion.wz0), channel_id=1, source_target_pairs={{0,24},{8,16},{16,8},{24,0},{1,25},{9,17},{17,9},{25,1},{2,26},{10... | collective-permute-start | bytes 589832 | tf_op jit(solution)/shard_map/ppermute | solution.py:366
  5.8 9.8 %collective-permute-start.4 = (bf16[12,64,128]{2,1,0:T(8,128)(2,1)S(1)}, bf16[12,64,128]{2,1,0:T(8,128)(2,1)S(1)}, u32[]{:S(2)}, u32[]{:S(2)}) collective-permute-start(bf16[12,64,128]{2,1,0:T(8,128)(2,1)S(1)} %pad_maximum_fusion.wz0), channel_id=1, source_target_pairs={{0,16},{8,24},{16,0},{24,8},{1,17},{9,25},{17,1},{25,9},{2,18},{10... | collective-permute-start | bytes 589832 | tf_op jit(solution)/shard_map/ppermute | solution.py:366
  6.3 9.5 %collective-permute-start.3 = (bf16[12,64,128]{2,1,0:T(8,128)(2,1)S(1)}, bf16[12,64,128]{2,1,0:T(8,128)(2,1)S(1)}, u32[]{:S(2)}, u32[]{:S(2)}) collective-permute-start(bf16[12,64,128]{2,1,0:T(8,128)(2,1)S(1)} %pad_maximum_fusion.wz0), channel_id=1, source_target_pairs={{0,8},{8,0},{16,24},{24,16},{1,9},{9,1},{17,25},{25,17},{2,10},{10... | collective-permute-start | bytes 589832 | tf_op jit(solution)/shard_map/ppermute | solution.py:366
  6.4 4.3 %collective-permute-start.1 = (bf16[2,32,128]{2,1,0:T(8,128)(2,1)S(1)}, bf16[2,32,128]{2,1,0:T(8,128)(2,1)S(1)}, u32[]{:S(2)}, u32[]{:S(2)}) collective-permute-start(bf16[2,32,128]{2,1,0:T(8,128)(2,1)S(1)} %pad_maximum_fusion.2), channel_id=1, source_target_pairs={{0,2},{1,3},{2,0},{3,1},{4,6},{5,7},{6,4},{7,5},{8,10},{9,11},{10,... | collective-permute-start | bytes 49160 | tf_op jit(solution)/shard_map/ppermute | solution.py:366
  9.1 1.0 %copy-start = (bf16[1,12,512,32]{2,3,1,0:T(8,128)(2,1)S(1)}, bf16[1,12,512,32]{2,3,1,0:T(8,128)(2,1)}, u32[]{:S(2)}) copy-start(bf16[1,12,512,32]{2,3,1,0:T(8,128)(2,1)} %param.13) | copy-start | bytes 1179652
  10.7 4.9 %collective-permute-start.2 = (bf16[4,32,128]{2,1,0:T(8,128)(2,1)S(1)}, bf16[4,32,128]{2,1,0:T(8,128)(2,1)S(1)}, u32[]{:S(2)}, u32[]{:S(2)}) collective-permute-start(bf16[4,32,128]{2,1,0:T(8,128)(2,1)S(1)} %pad_maximum_fusion.1.near), channel_id=1, source_target_pairs={{0,4},{1,5},{2,6},{3,7},{4,0},{5,1},{6,2},{7,3},{8,12},{9,13},{10,... | collective-permute-start | bytes 98312 | tf_op jit(solution)/shard_map/ppermute | solution.py:366

commit v6 on v5

--- a/solution.py
+++ b/solution.py
@@ -214,6 +214,8 @@
     def later(t):
         imaged[t] = dot(head, mix_parts[t])
         right_parts[t] = right_64(dot(right_rows[t], below(right_rows[t], right_rows[t]), NT) + identity)
+
+    def turned(t):
         left_columns[t] = jnp.transpose(below(left_rows[t], left_rows[t]))
 
     inverse_factors(wide_rows, factors, rank, [functools.partial(later, t) for t in every])
@@ -233,7 +235,7 @@
                 beside(high, middle, pick(64, high, low)), wide_right(basis[t]), NT
             )
         if step < ITERS - 1:
-            inverse_factors(rows, factors)
+            inverse_factors(rows, factors, 0, [functools.partial(turned, t) for t in every[step * 6 : step * 6 + 6]])
             for t in every:
                 imaged[t] = dot(inverse(t).astype(BF16)[:, :96], image_parts[t])
 

time: 29.4 us -> 29.4 us (level)
  no operation moved by 1% of the time
where the time goes in v6:
time: 29.4 us; the launch traced here: 29 us
  Pallas kernels  14.7 us (50%)
  starting transfers between devices  9.31 us (32%)
  other arithmetic  3.28 us (11%)
  local copies, waits for them, and re-layouts  1 us (3%)
  waiting for transfers between devices  0.72 us (2%)
    pallas_call x1, Pallas kernels, local_step(): pl.pallas_call(functools.partial(kernel, place), out_shape=jax.ShapeDtype...  13.2 us
    ppermute x6, starting transfers between devices, swap(): return lax.ppermute(x, axis, [(i, i ^ step) for i in range(size)])  9.31 us
    unnamed x2, local copies, waits for them, and re-layouts  1 us
    concatenate x1, other arithmetic, shards(): wz = jnp.concatenate([turn(upper_inner), turn(upper_outer)], 1)  0.96 us
    concatenate x1, other arithmetic, shards(): start = jnp.concatenate([turn(start_block), turn(start_block)], 1)  0.87 us
    pallas_call x1, Pallas kernels, local_factors(): pl.pallas_call(inverse_factors, out_shape=jax.ShapeDtypeStruct((32 * SLOT...  0.84 us
    concatenate x1, other arithmetic, shards(): pair = jnp.concatenate([turn(panel_outer[0]), turn(panel_inner[0])], -1)  0.79 us
    ppermute x6, waiting for transfers between devices, swap(): return lax.ppermute(x, axis, [(i, i ^ step) for i in range(size)])  0.72 us
  transfers between devices with their start and end apart: 6, of which 2 were waited for; matrix products, arithmetic and copies ran while one was open for 5% of the time, Pallas kernels for 5%

profile of v6, /device:TPU:0, one launch (start us, length us, event | category | flops | bytes accessed | tf_op | source)
XLA Modules:
  0.0 29.0 jit_solution(9454351519595577851)
XLA Ops:
  0.0 0.8 %pad_maximum_fusion.4 = bf16[32,128]{1,0:T(8,128)(2,1)S(1)} fusion(bf16[32,64]{1,0:T(8,128)(2,1)} %bitcast.27, bf16[32,64]{1,0:T(8,128)(2,1)} %bitcast.28), kind=kLoop, calls=%fused_computation.4 | loop fusion | flops 16384 | bytes 16384 | tf_op jit(solution)/shard_map/concatenate | solution.py:380
  0.8 1.0 %pad_maximum_fusion.wz0 = bf16[12,64,128]{2,1,0:T(8,128)(2,1)S(1)} fusion(bf16[12,32,128]{2,1,0:T(8,128)(2,1)} %bitcast.23, bf16[12,32,128]{2,1,0:T(8,128)(2,1)} %bitcast.24), kind=kLoop, calls=%fused_computation | loop fusion | flops 393216 | bytes 393216 | tf_op jit(solution)/shard_map/concatenate | solution.py:381
  1.8 0.5 %collective-permute-start = (bf16[32,128]{1,0:T(8,128)(2,1)S(1)}, bf16[32,128]{1,0:T(8,128)(2,1)S(1)}, u32[]{:S(2)}, u32[]{:S(2)}) collective-permute-start(bf16[32,128]{1,0:T(8,128)(2,1)S(1)} %pad_maximum_fusion.4), channel_id=1, source_target_pairs={{0,1},{1,0},{2,3},{3,2},{4,5},{5,4},{6,7},{7,6},{8,9},{9,8},{10,11... | collective-permute-start | bytes 24584 | tf_op jit(solution)/shard_map/ppermute | solution.py:368
  2.3 3.5 %collective-permute-start.5 = (bf16[12,64,128]{2,1,0:T(8,128)(2,1)S(1)}, bf16[12,64,128]{2,1,0:T(8,128)(2,1)S(1)}, u32[]{:S(2)}, u32[]{:S(2)}) collective-permute-start(bf16[12,64,128]{2,1,0:T(8,128)(2,1)S(1)} %pad_maximum_fusion.wz0), channel_id=1, source_target_pairs={{0,24},{8,16},{16,8},{24,0},{1,25},{9,17},{17,9},{25,1},{2,26},{10... | collective-permute-start | bytes 589832 | tf_op jit(solution)/shard_map/ppermute | solution.py:368
  5.8 0.5 %collective-permute-start.4 = (bf16[12,64,128]{2,1,0:T(8,128)(2,1)S(1)}, bf16[12,64,128]{2,1,0:T(8,128)(2,1)S(1)}, u32[]{:S(2)}, u32[]{:S(2)}) collective-permute-start(bf16[12,64,128]{2,1,0:T(8,128)(2,1)S(1)} %pad_maximum_fusion.wz0), channel_id=1, source_target_pairs={{0,16},{8,24},{16,0},{24,8},{1,17},{9,25},{17,1},{25,9},{2,18},{10... | collective-permute-start | bytes 589832 | tf_op jit(solution)/shard_map/ppermute | solution.py:368
  6.3 0.1 collective-permute-start.3
  6.4 0.0 collective-permute-done
  6.4 2.0 %collective-permute-start.1 = (bf16[2,32,128]{2,1,0:T(8,128)(2,1)S(1)}, bf16[2,32,128]{2,1,0:T(8,128)(2,1)S(1)}, u32[]{:S(2)}, u32[]{:S(2)}) collective-permute-start(bf16[2,32,128]{2,1,0:T(8,128)(2,1)S(1)} %pad_maximum_fusion.2), channel_id=1, source_target_pairs={{0,2},{1,3},{2,0},{3,1},{4,6},{5,7},{6,4},{7,5},{8,10},{9,11},{10,... | collective-permute-start | bytes 49160 | tf_op jit(solution)/shard_map/ppermute | solution.py:368
  8.4 0.7 %compare_convert_fusion.flags = s32[1,12]{1,0:T(1,128)S(1)} fusion(s32[1,12]{1,0:T(1,128)} %param.16), kind=kLoop, calls=%fused_computation.5 | loop fusion | flops 24 | bytes 96 | tf_op jit(solution)/shard_map/convert_element_type | solution.py:400
  9.1 0.0 copy-start
  9.1 1.0 %copy-done = bf16[1,12,512,32]{2,3,1,0:T(8,128)(2,1)S(1)} copy-done((bf16[1,12,512,32]{2,3,1,0:T(8,128)(2,1)S(1)}, bf16[1,12,512,32]{2,3,1,0:T(8,128)(2,1)}, u32[]{:S(2)}) %copy-start) | copy-done | bytes 393240
  10.1 0.6 %shard_map.91.rows_ref = f32[512,128]{1,0:T(8,128)S(1)} custom-call(bf16[12,32,512]{2,1,0:T(8,128)(2,1)S(1)} %bitcast.20), custom_call_target="tpu_custom_call" | custom-call | tf_op jit(solution)/shard_map/pallas_call | solution.py:300
  10.7 0.0 collective-permute-done.1
  10.7 2.7 %collective-permute-start.2 = (bf16[4,32,128]{2,1,0:T(8,128)(2,1)S(1)}, bf16[4,32,128]{2,1,0:T(8,128)(2,1)S(1)}, u32[]{:S(2)}, u32[]{:S(2)}) collective-permute-start(bf16[4,32,128]{2,1,0:T(8,128)(2,1)S(1)} %pad_maximum_fusion.1.near), channel_id=1, source_target_pairs={{0,4},{1,5},{2,6},{3,7},{4,0},{5,1},{6,2},{7,3},{8,12},{9,13},{10,... | collective-permute-start | bytes 98312 | tf_op jit(solution)/shard_map/ppermute | solution.py:368
  13.4 0.9 %pad_maximum_fusion.3.start = f32[32,128]{1,0:T(8,128)S(1)} fusion(f32[32,64]{1,0:T(8,128)} %bitcast.26), kind=kLoop, calls=%fused_computation.3 | loop fusion | flops 4096 | bytes 24576 | tf_op jit(solution)/shard_map/concatenate | solution.py:401
  14.3 0.8 %shard_map.92.first_factors = f32[512,128]{1,0:T(8,128)S(1)} custom-call(f32[512,128]{1,0:T(8,128)S(1)} %shard_map.91.rows_ref), custom_call_target="tpu_custom_call" | custom-call | tf_op jit(solution)/shard_map/pallas_call | solution.py:311
  15.1 0.5 %collective-permute-done.2.far = bf16[4,32,128]{2,1,0:T(8,128)(2,1)S(1)} collective-permute-done((bf16[4,32,128]{2,1,0:T(8,128)(2,1)S(1)}, bf16[4,32,128]{2,1,0:T(8,128)(2,1)S(1)}, u32[]{:S(2)}, u32[]{:S(2)}) %collective-permute-start.2) | collective-permute-done | bytes 32800 | tf_op jit(solution)/shard_map/ppermute | solution.py:368
  15.6 0.0 collective-permute-done.5.wz3
  15.6 0.0 collective-permute-done.4.wz2
  15.6 0.2 collective-permute-done.3.wz1
  15.8 13.2 %shard_map.93 = bf16[12,512,512]{2,1,0:T(8,128)(2,1)} custom-call(bf16[4,32,128]{2,1,0:T(8,128)(2,1)S(1)} %pad_maximum_fusion.1.near, bf16[4,32,128]{2,1,0:T(8,128)(2,1)S(1)} %collective-permute-done.2.far, f32[512,128]{1,0:T(8,128)S(1)} %shard_map.92.first_factors, s32[1,12]{1,0:T(1,128)S(1)} %compare_convert_fusion.flags, ...), custom_call_target="tpu_custom_call" | custom-call | tf_op jit(solution)/shard_map/pallas_call | solution.py:330
  (2 shorter events, 0.0 us)
Async XLA Ops:
  1.8 4.7 %collective-permute-start = (bf16[32,128]{1,0:T(8,128)(2,1)S(1)}, bf16[32,128]{1,0:T(8,128)(2,1)S(1)}, u32[]{:S(2)}, u32[]{:S(2)}) collective-permute-start(bf16[32,128]{1,0:T(8,128)(2,1)S(1)} %pad_maximum_fusion.4), channel_id=1, source_target_pairs={{0,1},{1,0},{2,3},{3,2},{4,5},{5,4},{6,7},{7,6},{8,9},{9,8},{10,11... | collective-permute-start | bytes 24584 | tf_op jit(solution)/shard_map/ppermute | solution.py:368
  2.3 13.3 %collective-permute-start.5 = (bf16[12,64,128]{2,1,0:T(8,128)(2,1)S(1)}, bf16[12,64,128]{2,1,0:T(8,128)(2,1)S(1)}, u32[]{:S(2)}, u32[]{:S(2)}) collective-permute-start(bf16[12,64,128]{2,1,0:T(8,128)(2,1)S(1)} %pad_maximum_fusion.wz0), channel_id=1, source_target_pairs={{0,24},{8,16},{16,8},{24,0},{1,25},{9,17},{17,9},{25,1},{2,26},{10... | collective-permute-start | bytes 589832 | tf_op jit(solution)/shard_map/ppermute | solution.py:368
  5.8 9.8 %collective-permute-start.4 = (bf16[12,64,128]{2,1,0:T(8,128)(2,1)S(1)}, bf16[12,64,128]{2,1,0:T(8,128)(2,1)S(1)}, u32[]{:S(2)}, u32[]{:S(2)}) collective-permute-start(bf16[12,64,128]{2,1,0:T(8,128)(2,1)S(1)} %pad_maximum_fusion.wz0), channel_id=1, source_target_pairs={{0,16},{8,24},{16,0},{24,8},{1,17},{9,25},{17,1},{25,9},{2,18},{10... | collective-permute-start | bytes 589832 | tf_op jit(solution)/shard_map/ppermute | solution.py:368
  6.3 9.5 %collective-permute-start.3 = (bf16[12,64,128]{2,1,0:T(8,128)(2,1)S(1)}, bf16[12,64,128]{2,1,0:T(8,128)(2,1)S(1)}, u32[]{:S(2)}, u32[]{:S(2)}) collective-permute-start(bf16[12,64,128]{2,1,0:T(8,128)(2,1)S(1)} %pad_maximum_fusion.wz0), channel_id=1, source_target_pairs={{0,8},{8,0},{16,24},{24,16},{1,9},{9,1},{17,25},{25,17},{2,10},{10... | collective-permute-start | bytes 589832 | tf_op jit(solution)/shard_map/ppermute | solution.py:368
  6.4 4.3 %collective-permute-start.1 = (bf16[2,32,128]{2,1,0:T(8,128)(2,1)S(1)}, bf16[2,32,128]{2,1,0:T(8,128)(2,1)S(1)}, u32[]{:S(2)}, u32[]{:S(2)}) collective-permute-start(bf16[2,32,128]{2,1,0:T(8,128)(2,1)S(1)} %pad_maximum_fusion.2), channel_id=1, source_target_pairs={{0,2},{1,3},{2,0},{3,1},{4,6},{5,7},{6,4},{7,5},{8,10},{9,11},{10,... | collective-permute-start | bytes 49160 | tf_op jit(solution)/shard_map/ppermute | solution.py:368
  9.1 1.0 %copy-start = (bf16[1,12,512,32]{2,3,1,0:T(8,128)(2,1)S(1)}, bf16[1,12,512,32]{2,3,1,0:T(8,128)(2,1)}, u32[]{:S(2)}) copy-start(bf16[1,12,512,32]{2,3,1,0:T(8,128)(2,1)} %param.13) | copy-start | bytes 1179652
  10.7 4.9 %collective-permute-start.2 = (bf16[4,32,128]{2,1,0:T(8,128)(2,1)S(1)}, bf16[4,32,128]{2,1,0:T(8,128)(2,1)S(1)}, u32[]{:S(2)}, u32[]{:S(2)}) collective-permute-start(bf16[4,32,128]{2,1,0:T(8,128)(2,1)S(1)} %pad_maximum_fusion.1.near), channel_id=1, source_target_pairs={{0,4},{1,5},{2,6},{3,7},{4,0},{5,1},{6,2},{7,3},{8,12},{9,13},{10,... | collective-permute-start | bytes 98312 | tf_op jit(solution)/shard_map/ppermute | solution.py:368
